TPU v7x, 256 devices: a whole 4x4x8 slice. The times are simulated.
256 devices in a mesh: replica: 64 (over z_lo, x, y), tensor: 4 (over z_hi, core).
Axes of the slice: x: 4, y: 4, z: 8 (z_hi: 2, z_lo: 4; z = z_hi * 4 + z_lo), core: 2. Of those that a mesh axis runs over, the one named last changes fastest.
Arguments:
- hidden: bfloat16 [128, 4096], P('replica'), may hold values from -6 to 6
- queries: bfloat16 [128, 2048], P('replica', 'tensor'), may hold values from -1.73 to 1.73
- new_key: bfloat16 [128, 2048], P('replica', 'tensor'), may hold values from -6 to 6
- new_value: bfloat16 [128, 2048], P('replica', 'tensor'), may hold values from -6 to 6
- cache_keys: bfloat16 [128, 768, 2048], P('replica', None, 'tensor'), may hold values from -35 to 35
- cache_values: bfloat16 [128, 768, 2048], P('replica', None, 'tensor'), may hold values from -6 to 6
- w_out: bfloat16 [2048, 4096], P('tensor'), may hold values from -0.5 to 0.5
- lengths: int32 [128], replicated, may hold values from 16 to 767
- moved_slot: int32 [64], replicated, may hold values from -1 to 1, as said below
Outputs:
- layer_out: bfloat16 [128, 4096], P('replica', 'tensor')
- keys_out: bfloat16 [128, 768, 2048], P('replica', None, 'tensor')
- values_out: bfloat16 [128, 768, 2048], P('replica', None, 'tensor')
Inputs may be any that keep to these rules, and one draw needn't show every extreme that they name: moved_slot[r] is -1 exactly when moved_slot[(r + 32) mod 64] is -1.
All inputs are finite; a program needn't handle non-finite values.
Results may differ from a plain program's by a relative error of at most 0.0053.
Values may be sent and summed in bfloat16 or wider, within the bound.
A program may use at most 64 MiB of HBM per device.

v0:
```python
import jax
import jax.numpy as jnp
from jax import lax
from jax.sharding import PartitionSpec as P

HEAD_DIM = 128


def swapped(block, axis, distance):
    count = lax.axis_size(axis)
    route = []
    for low in range(count):
        high = low | 1 << distance
        if high != low and high < count:
            route += [(low, high), (high, low)]
    return lax.ppermute(block, axis, route)


def append_token(cache, fresh, row_lengths):
    positions = lax.broadcasted_iota(jnp.int32, cache.shape, 1)
    length_bound = row_lengths[:, None, None]
    return jnp.where(
        positions < length_bound,
        cache,
        jnp.where(positions == length_bound, fresh[:, None, :], jnp.zeros_like(cache)),
    )


def attend(queries, key_rows, value_rows, row_lengths):
    slot_count, capacity, row_width = key_rows.shape
    head_count = row_width // HEAD_DIM
    q_split = queries.reshape(slot_count, head_count, HEAD_DIM)
    k_split = key_rows.reshape(slot_count, capacity, head_count, HEAD_DIM)
    v_split = value_rows.reshape(slot_count, capacity, head_count, HEAD_DIM)
    scores = jnp.einsum(
        "shd,schd->shc", q_split, k_split, preferred_element_type=jnp.float32
    ) * HEAD_DIM ** (-0.5)
    positions = lax.broadcasted_iota(jnp.int32, scores.shape, 2)
    scores = jnp.where(positions <= row_lengths[:, None, None], scores, -1e30)
    peak_score = jnp.max(scores, axis=2, keepdims=True)
    exp_terms = jnp.exp(scores - peak_score)
    weights = (exp_terms / jnp.sum(exp_terms, axis=2, keepdims=True)).astype(jnp.bfloat16)
    attended = jnp.einsum("shc,schd->shd", weights, v_split, preferred_element_type=jnp.float32)
    return attended.reshape(slot_count, row_width).astype(jnp.bfloat16)


def head_terms(w_out, attended):
    return lax.dot_general(
        w_out, attended, (((0,), (1,)), ((), ())), preferred_element_type=jnp.float32
    )


def take_slot(buffer, slot_index):
    return lax.dynamic_index_in_dim(buffer, slot_index, 0, keepdims=False)


def place_row(buffer, arriving, slot_index, accept):
    current = take_slot(buffer, slot_index)
    chosen = jnp.where(accept, arriving, current)
    return lax.dynamic_update_index_in_dim(buffer, chosen, slot_index, 0)


def carry_cache(key_rows, value_rows, outgoing, accept, pair_bit):
    key_row = take_slot(key_rows, outgoing)
    value_row = take_slot(value_rows, outgoing)
    arriving = swapped((key_row, value_row), "replica", pair_bit)
    key_in, value_in = (arriving[0], arriving[1])
    key_rows = place_row(key_rows, key_in, outgoing, accept)
    value_rows = place_row(value_rows, value_in, outgoing, accept)
    return (key_rows, value_rows)


def shards(
    hidden, queries, new_key, new_value, cache_keys, cache_values, w_out, lengths, moved_slot
):
    slot_dev = hidden.shape[0]
    replicas = lax.axis_size("replica")
    replica_index = lax.axis_index("replica")
    pair_bit = replicas.bit_length() - 2
    partner = (replica_index + replicas // 2) % replicas
    own_lengths = lax.dynamic_slice_in_dim(lengths, replica_index * slot_dev, slot_dev)
    leaving_slot = moved_slot[replica_index]
    partner_leaving = moved_slot[partner]
    outgoing = jnp.maximum(leaving_slot, 0)
    accept = leaving_slot >= 0
    partner_length = lengths[partner * slot_dev + jnp.maximum(partner_leaving, 0)]
    slot_iota = lax.broadcasted_iota(jnp.int32, (slot_dev,), 0)
    lengths_here = jnp.where(slot_iota == leaving_slot, partner_length, own_lengths)
    key_rows = append_token(cache_keys, new_key, own_lengths)
    value_rows = append_token(cache_values, new_value, own_lengths)
    pieces = lax.axis_size("tensor")
    column_share = w_out.shape[1] // pieces
    column_start = lax.axis_index("tensor") * column_share
    moved_keys, moved_values = carry_cache(key_rows, value_rows, outgoing, accept, pair_bit)
    arriving = swapped(
        (take_slot(queries, outgoing), take_slot(hidden, outgoing)), "replica", pair_bit
    )
    queries_here = place_row(queries, arriving[0], outgoing, accept)
    hidden_here = place_row(hidden, arriving[1], outgoing, accept)
    attended = attend(queries_here, moved_keys, moved_values, lengths_here)
    branch = lax.psum_scatter(
        head_terms(w_out, attended), "tensor", scatter_dimension=0, tiled=True
    ).T
    residual_part = lax.dynamic_slice_in_dim(hidden_here, column_start, column_share, 1)
    layer_out = (residual_part.astype(jnp.float32) + branch).astype(jnp.bfloat16)
    return (layer_out, moved_keys, moved_values)


def solution(mesh):
    return jax.shard_map(
        shards,
        mesh=mesh,
        in_specs=(
            P("replica", None),
            P("replica", "tensor"),
            P("replica", "tensor"),
            P("replica", "tensor"),
            P("replica", None, "tensor"),
            P("replica", None, "tensor"),
            P("tensor", None),
            P(),
            P(),
        ),
        out_specs=(
            P("replica", "tensor"),
            P("replica", None, "tensor"),
            P("replica", None, "tensor"),
        ),
        check_vma=False,
    )
```

profile of v0, /device:TPU:24, one launch (start us, length us, event | category | flops | bytes accessed | tf_op | source)
XLA Modules:
  0.0 169.1 jit_solution(12948064400982801291)
XLA Ops:
  7.2 0.0 reduce-scatter.4.cloned.1.call-start
  7.2 0.7 copy.46
  7.9 0.7 copy.45
  8.6 1.3 fusion.26
  11.2 1.2 dynamic_slice.38
  12.5 2.0 %compare_select_fusion = (s32[2]{0:T(128)S(1)}, s32[2]{0:T(128)S(1)}) fusion(s32[]{:T(128)} %bitcast.2, s32[]{:T(128)} %bitcast, s32[128]{0:T(128)} %param.16, s32[]{:T(128)S(6)} %select_n.97), kind=kLoop, calls=%fused_computation.37 | loop fusion | flops 4 | bytes 36 | tf_op jit(solution)/shard_map/jit(_where)/select_n | solution.py:88
  14.5 3.3 %fusion.5 = (bf16[2,768,512]{2,1,0:T(8,128)(2,1)S(1)}, bf16[2,768,512]{2,1,0:T(8,128)(2,1)S(1)}) fusion(bf16[2,768,512]{2,1,0:T(8,128)(2,1)} %param.13, s32[2]{0:T(128)S(1)} %get-tuple-element.4, bf16[2,512]{1,0:T(2,128)(2,1)} %param.11, bf16[2,768,512]{2,1,0:T(8,128)(2,1)} %param.14, bf16[2,512]{1,0:T(2,128)(2,1)} %param.12), kind=kLoop, calls=%fused_computation.8 | loop fusion | flops 4718592 | bytes 6295560 | tf_op jit(solution)/shard_map/jit(_where)/select_n | solution.py:22
  17.8 0.0 copy-start.1
  17.9 0.1 dynamic-slice_bitcast_fusion.1
  17.9 3.4 %collective-permute-start.2 = (bf16[768,512]{1,0:T(8,128)(2,1)S(1)}, bf16[768,512]{1,0:T(8,128)(2,1)S(1)}, u32[]{:S(2)}, u32[]{:S(2)}) collective-permute-start(bf16[768,512]{1,0:T(8,128)(2,1)S(1)} %dynamic-slice_bitcast_fusion.1), channel_id=1, source_target_pairs={{0,128},{128,0},{4,132},{132,4},{8,136},{136,8},{12,140},{140,12},... | collective-permute-start | bytes 2359304 | tf_op jit(solution)/shard_map/ppermute | solution.py:16
  21.3 0.9 dynamic-slice_bitcast_fusion
  22.2 0.0 copy-done.1
  22.2 0.3 collective-permute-start.3
  22.5 2.7 %collective-permute-start.1 = (bf16[512]{0:T(512)(128)(2,1)S(1)}, bf16[512]{0:T(512)(128)(2,1)S(1)}, u32[]{:S(2)}, u32[]{:S(2)}) collective-permute-start(bf16[512]{0:T(512)(128)(2,1)S(1)} %dynamic-slice_reduce_fusion.1), channel_id=1, source_target_pairs={{0,128},{128,0},{4,132},{132,4},{8,136},{136,8},{12,140},{140,12},... | collective-permute-start | bytes 3080 | tf_op jit(solution)/shard_map/ppermute | solution.py:16
  25.2 0.1 dynamic-slice_reduce_fusion
  25.3 0.4 collective-permute-start
  26.3 63.4 %collective-permute-done.1 = bf16[512]{0:T(512)(128)(2,1)S(1)} collective-permute-done((bf16[512]{0:T(512)(128)(2,1)S(1)}, bf16[512]{0:T(512)(128)(2,1)S(1)}, u32[]{:S(2)}, u32[]{:S(2)}) %collective-permute-start.1) | collective-permute-done | bytes 1056 | tf_op jit(solution)/shard_map/ppermute | solution.py:16
  89.9 0.0 collective-permute-done.2
  89.9 0.2 bitcast_dynamic-update-slice_fusion.1
  90.1 0.0 copy-start
  90.1 0.7 copy.18
  90.8 0.4 copy-done
  91.3 0.3 fusion.29
  91.6 0.2 fusion.13
  91.8 0.0 collective-permute-done.3
  91.8 2.2 %bitcast_dynamic-update-slice_fusion = bf16[2,768,512]{2,1,0:T(8,128)(2,1)} fusion(bf16[2,768,512]{2,1,0:T(8,128)(2,1)} %copy-done.1, s32[]{:T(128)S(6)} %max.9, bf16[768,512]{1,0:T(8,128)(2,1)} %collective-permute-done.3, bf16[768,512]{1,0:T(8,128)(2,1)} %dynamic-slice_bitcast_fusion, pred[]{:T(512)S(6)} %ge.3), kind=kLoop, calls=%fused_computation.17 | loop fusion | flops 393216 | bytes 2359301 | tf_op jit(solution)/shard_map/jit(dynamic_update_index_in_dim)/dynamic_update_slice | solution.py:60
  94.1 1.7 %fusion.6 = f32[2,4,1,128]{3,2,1,0:T(1,128)S(1)} fusion(bf16[2,4,768,1]{2,1,0,3:T(4,128)(2,1)S(1)} %fusion.13, bf16[2,768,512]{2,1,0:T(8,128)(2,1)} %bitcast_dynamic-update-slice_fusion), kind=kOutput, calls=%fused_computation.9 | convolution fusion | flops 1572864 | bytes 1589248 | tf_op jit(solution)/shard_map/shc,schd->shd/dot_general | solution.py:43
  95.8 2.9 %convolution_bitcast_fusion = f32[4096,2]{0,1:T(2,128)S(1)} fusion(bf16[512,4096]{1,0:T(8,128)(2,1)} %param.15, bf16[1,2,4,128]{3,2,1,0:T(4,128)(2,1)S(1)} %convert_bitcast_fusion), kind=kOutput, calls=%fused_computation.2 | convolution fusion | flops 8388608 | bytes 4229120 | tf_op jit(solution)/shard_map/dot_general | solution.py:48
  98.6 2.0 %copy.19 = f32[4096,2]{1,0:T(8,128)} copy(f32[4096,2]{0,1:T(2,128)S(1)} %convolution_bitcast_fusion) | data formatting | bytes 65536
  100.7 0.0 reduce-scatter.4.cloned.1.call-update
  100.7 0.0 collective-permute-done
  100.7 0.1 dynamic_update_slice.15
  100.9 59.6 %reduce-scatter.4.cloned.1.call-done = f32[1024,2]{1,0:T(8,128)} async-done(((f32[4096,2]{1,0:T(8,128)}), f32[1024,2]{1,0:T(8,128)}) %reduce-scatter.4.cloned.1.call-update) | async-done | bytes 8208
  160.5 1.2 copy.20
  161.7 0.6 fusion.21
  (8 shorter events, 0.1 us)
Async XLA Ops:
  7.2 153.3 %reduce-scatter.4.cloned.1.call-start = ((), (), s32[]{:S(2)}) async-start(), calls=%async_computation.1 | async-start | bytes 2621440
  17.8 4.4 %copy-start.1 = (bf16[2,768,512]{2,1,0:T(8,128)(2,1)}, bf16[2,768,512]{2,1,0:T(8,128)(2,1)S(1)}, u32[]{:S(2)}) copy-start(bf16[2,768,512]{2,1,0:T(8,128)(2,1)S(1)} %get-tuple-element.6) | copy-start | bytes 4718596
  17.9 71.9 %collective-permute-start.2 = (bf16[768,512]{1,0:T(8,128)(2,1)S(1)}, bf16[768,512]{1,0:T(8,128)(2,1)S(1)}, u32[]{:S(2)}, u32[]{:S(2)}) collective-permute-start(bf16[768,512]{1,0:T(8,128)(2,1)S(1)} %dynamic-slice_bitcast_fusion.1), channel_id=1, source_target_pairs={{0,128},{128,0},{4,132},{132,4},{8,136},{136,8},{12,140},{140,12},... | collective-permute-start | bytes 2359304 | tf_op jit(solution)/shard_map/ppermute | solution.py:16
  22.2 69.6 %collective-permute-start.3 = (bf16[768,512]{1,0:T(8,128)(2,1)}, bf16[768,512]{1,0:T(8,128)(2,1)}, u32[]{:S(2)}, u32[]{:S(2)}) collective-permute-start(bf16[768,512]{1,0:T(8,128)(2,1)} %dynamic-slice_bitcast_fusion), channel_id=1, source_target_pairs={{0,128},{128,0},{4,132},{132,4},{8,136},{136,8},{12,140},{140,12},... | collective-permute-start | bytes 2359304 | tf_op jit(solution)/shard_map/ppermute | solution.py:16
  22.5 67.2 %collective-permute-start.1 = (bf16[512]{0:T(512)(128)(2,1)S(1)}, bf16[512]{0:T(512)(128)(2,1)S(1)}, u32[]{:S(2)}, u32[]{:S(2)}) collective-permute-start(bf16[512]{0:T(512)(128)(2,1)S(1)} %dynamic-slice_reduce_fusion.1), channel_id=1, source_target_pairs={{0,128},{128,0},{4,132},{132,4},{8,136},{136,8},{12,140},{140,12},... | collective-permute-start | bytes 3080 | tf_op jit(solution)/shard_map/ppermute | solution.py:16
  25.3 75.4 %collective-permute-start = (bf16[4096]{0:T(1024)(128)(2,1)S(1)}, bf16[4096]{0:T(1024)(128)(2,1)S(1)}, u32[]{:S(2)}, u32[]{:S(2)}) collective-permute-start(bf16[4096]{0:T(1024)(128)(2,1)S(1)} %dynamic-slice_reduce_fusion), channel_id=1, source_target_pairs={{0,128},{128,0},{4,132},{132,4},{8,136},{136,8},{12,140},{140,12},... | collective-permute-start | bytes 24584 | tf_op jit(solution)/shard_map/ppermute | solution.py:16
  90.1 1.1 copy-start
Sparse Core Ops, SparseCore 0:
  100.8 59.6 reduce-scatter.3
where the time goes:
time: 171 us; the launch traced here: 169 us
  waiting for transfers between devices  123 us (72%)
  between operations  16.1 us (9%)
  local copies, waits for them, and re-layouts  9.6 us (6%)
  other arithmetic  8.73 us (5%)
  starting transfers between devices  6.79 us (4%)
  matrix products  4.87 us (3%)
    ppermute x4, waiting for transfers between devices, swapped(): return lax.ppermute(block, axis, route)  63.4 us
    unnamed x2, waiting for transfers between devices  59.6 us
    ppermute x4, starting transfers between devices, swapped(): return lax.ppermute(block, axis, route)  6.75 us
    unnamed x8, local copies, waits for them, and re-layouts  5.07 us
  transfers between devices with their start and end apart: 5, of which 2 were waited for; matrix products, arithmetic and copies ran while one was open for 7% of the time, Pallas kernels for 0%

commit v1 on v0

v1 whole, which is shorter than its diff:
```python
import functools

import jax
import jax.numpy as jnp
from jax import lax
from jax.experimental import pallas as pl
from jax.experimental.pallas import tpu as pltpu
from jax.sharding import PartitionSpec as P

HEAD_DIM = 128
TILE = 16
LANES = 256
MESH = pl.DeviceIdType.MESH


def block_diagonal(row, heads):
    width = row.shape[1]
    row_id = lax.broadcasted_iota(jnp.int32, (8, width), 0)
    col_id = lax.broadcasted_iota(jnp.int32, (8, width), 1)
    own = (col_id >= row_id * HEAD_DIM) & (col_id < row_id * HEAD_DIM + HEAD_DIM)
    return own, jnp.where(own, jnp.broadcast_to(row, (8, width)), 0.0)


def attend_row(query, fresh_key, fresh_value, keys_ref, values_ref, length):
    cap, width = keys_ref.shape
    own, query_block = block_diagonal(query, width // HEAD_DIM)
    scale = HEAD_DIM**-0.5
    scores = lax.dot_general(
        query_block.astype(jnp.bfloat16), keys_ref[...], (((1,), (1,)), ((), ())), preferred_element_type=jnp.float32
    )
    scores = scores * scale
    fresh_score = jnp.sum(query_block * fresh_key, axis=1, keepdims=True) * scale
    position = lax.broadcasted_iota(jnp.int32, scores.shape, 1)
    live = position < length
    peak = jnp.maximum(jnp.max(jnp.where(live, scores, -1e30), axis=1, keepdims=True), fresh_score)
    terms = jnp.where(live, jnp.exp(jnp.minimum(scores - peak, 0.0)), 0.0)
    fresh_term = jnp.exp(fresh_score - peak)
    total = jnp.sum(terms, axis=1, keepdims=True) + fresh_term
    weights = (terms / total).astype(jnp.bfloat16)
    fresh_weight = (fresh_term / total).astype(jnp.bfloat16).astype(jnp.float32)
    mixed = lax.dot_general(
        weights, values_ref[...], (((1,), (0,)), ((), ())), preferred_element_type=jnp.float32
    )
    mixed = mixed + fresh_weight * fresh_value
    return jnp.sum(jnp.where(own, mixed, 0.0), axis=0, keepdims=True)


def as_rows(two_rows):
    pieces = [two_rows[s : s + 1, j * 128 : (j + 1) * 128] for s in range(2) for j in range(8)]
    return jnp.concatenate(pieces, axis=0)


def as_line(rows):
    return jnp.concatenate([rows[j : j + 1, :] for j in range(8)], axis=1)


def move_kernel(
    depth,
    lengths, moved, hidden, queries, new_key, new_value, cache_keys, cache_values, w_out,
    layer_out, arrived,
    keys, values, weights, outgoing, partial, partial_in,
    load_sem, weight_sem, move_send, move_recv, part_send, part_recv,
):
    replica = lax.axis_index("replica")
    tensor = lax.axis_index("tensor")
    partner = (replica + 32) % 64

    loads = []
    for kind, (source, held) in enumerate(((cache_keys, keys), (cache_values, values))):
        load = pltpu.make_async_copy(source, held, load_sem.at[kind])
        load.start()
        loads.append(load)
    weight_load = pltpu.make_async_copy(w_out, weights, weight_sem)
    weight_load.start()

    peers = [(replica, (tensor + k) % 4) for k in range(1, 4)]
    peers += [(partner, (tensor + k) % 4) for k in range(4)]
    barrier = pltpu.get_barrier_semaphore()
    for peer in peers:
        pl.semaphore_signal(barrier, inc=1, device_id=peer, device_id_type=MESH)

    leaving = moved[replica]
    leaving_slot = jnp.maximum(leaving, 0)
    leaving_length = lengths[replica * 2 + leaving_slot]
    key_rows = new_key[...].astype(jnp.float32)
    value_rows = new_value[...].astype(jnp.float32)
    in_tile = lax.broadcasted_iota(jnp.int32, (TILE, LANES), 0)

    moves = []
    for quarter in range(4):
        kind, half = quarter // 2, quarter % 2
        held = (keys, values)[kind]
        fresh_rows = (key_rows, value_rows)[kind][:, half * LANES : (half + 1) * LANES]
        fresh = jnp.where(leaving_slot == 1, fresh_rows[1:2], fresh_rows[0:1])
        fresh = jnp.broadcast_to(fresh, (TILE, LANES))
        if half == 0:
            loads[kind].wait()

        def pack(step, carry, held=held, half=half, quarter=quarter, fresh=fresh):
            for j in range(4):
                block = step * 4 + j
                tile = held[leaving_slot, pl.ds(block * TILE, TILE), half * LANES : (half + 1) * LANES]
                position = in_tile + block * TILE
                tile = jnp.where(position < leaving_length, tile.astype(jnp.float32), fresh)
                outgoing[quarter * 4 + j, step] = tile.astype(jnp.bfloat16)
            return carry

        lax.fori_loop(0, depth, pack, 0)
        if quarter == 0:
            pl.semaphore_wait(barrier, len(peers))
        move = pltpu.make_async_remote_copy(
            src_ref=outgoing.at[quarter * 4 : quarter * 4 + 4, 0:depth],
            dst_ref=arrived.at[quarter * 4 : quarter * 4 + 4, 0:depth],
            send_sem=move_send.at[quarter],
            recv_sem=move_recv.at[quarter],
            device_id=(partner, tensor),
            device_id_type=MESH,
        )
        move.start()
        moves.append(move)

    query_rows = queries[...].astype(jnp.float32)
    attended = []
    for slot in range(2):
        attended.append(
            attend_row(
                query_rows[slot : slot + 1], key_rows[slot : slot + 1], value_rows[slot : slot + 1],
                keys.at[slot], values.at[slot], lengths[replica * 2 + slot],
            )
        )
    attended = jnp.concatenate(attended + [jnp.zeros((6, attended[0].shape[1]), jnp.float32)], axis=0)
    attended = attended.astype(jnp.bfloat16)

    weight_load.wait()
    for piece in range(4):
        product = jnp.dot(
            attended, weights[:, piece * 1024 : (piece + 1) * 1024], preferred_element_type=jnp.float32
        )
        partial[piece] = as_rows(product[0:2])
    residual = hidden[:, pl.ds(pl.multiple_of(tensor * 1024, 1024), 1024)].astype(jnp.float32)
    partial[tensor] = partial[tensor] + as_rows(residual)

    shares = []
    for k in range(8):
        if k == 0:
            continue
        piece = (tensor + k) % 4
        share = pltpu.make_async_remote_copy(
            src_ref=partial.at[piece],
            dst_ref=partial_in.at[k],
            send_sem=part_send.at[k],
            recv_sem=part_recv.at[k],
            device_id=((replica, partner)[k // 4], piece),
            device_id_type=MESH,
        )
        share.start()
        shares.append(share)
    for share in shares:
        share.wait()
    here = partial[tensor] + partial_in[1] + partial_in[2] + partial_in[3]
    there = partial_in[4] + partial_in[5] + partial_in[6] + partial_in[7]
    coming = jnp.where(moved[partner] == 1, there[8:16], there[0:8])
    lines = [
        as_line(jnp.where(leaving == slot, coming, here[slot * 8 : slot * 8 + 8])) for slot in range(2)
    ]
    layer_out[...] = jnp.concatenate(lines, axis=0).astype(jnp.bfloat16)

    for move in moves:
        move.wait()


def place_kernel(lengths, moved, new_key, new_value, cache_keys, cache_values, arrived, keys_out, values_out):
    chunk, slot = pl.program_id(0), pl.program_id(1)
    replica = lax.axis_index("replica")
    partner = (replica + 32) % 64
    rows = cache_keys.shape[1]
    comes = moved[replica] == slot
    length = lengths[replica * 2 + slot]
    arriving_length = lengths[partner * 2 + jnp.maximum(moved[partner], 0)]
    in_tile = lax.broadcasted_iota(jnp.int32, (TILE, LANES), 0)
    for kind, (fresh, source, target) in enumerate(
        ((new_key, cache_keys, keys_out), (new_value, cache_values, values_out))
    ):
        fresh_rows = fresh[...].astype(jnp.float32)
        fresh_row = jnp.where(slot == 1, fresh_rows[1:2], fresh_rows[0:1])
        for half in range(2):
            lanes = slice(half * LANES, (half + 1) * LANES)
            line = jnp.broadcast_to(fresh_row[:, lanes], (TILE, LANES))
            for block in range(rows // TILE):
                position = in_tile + (chunk * rows + block * TILE)
                span = slice(block * TILE, (block + 1) * TILE)
                own = source[0, span, lanes].astype(jnp.float32)
                own = jnp.where(position < length, own, jnp.where(position == length, line, 0.0))
                came = arrived[(kind * 2 + half) * 4 + block % 4, block // 4].astype(jnp.float32)
                came = jnp.where(position <= arriving_length, came, 0.0)
                target[0, span, lanes] = jnp.where(comes, came, own).astype(jnp.bfloat16)


def shards(
    hidden, queries, new_key, new_value, cache_keys, cache_values, w_out, lengths, moved_slot
):
    slots, cap, width = cache_keys.shape
    depth = cap // TILE // 4
    any_spec = pl.BlockSpec(memory_space=pl.ANY)
    vmem_spec = pl.BlockSpec(memory_space=pltpu.VMEM)
    smem_spec = pl.BlockSpec(memory_space=pltpu.SMEM)

    layer_out, arrived = pl.pallas_call(
        functools.partial(move_kernel, depth),
        out_shape=(
            jax.ShapeDtypeStruct((slots, w_out.shape[1] // 4), jnp.bfloat16),
            jax.ShapeDtypeStruct((16, cap // TILE // 4, TILE, LANES), jnp.bfloat16),
        ),
        in_specs=[smem_spec] * 2 + [vmem_spec] * 4 + [any_spec] * 3,
        out_specs=(vmem_spec, any_spec),
        scratch_shapes=[
            pltpu.VMEM((slots, cap, width), jnp.bfloat16),
            pltpu.VMEM((slots, cap, width), jnp.bfloat16),
            pltpu.VMEM(w_out.shape, jnp.bfloat16),
            pltpu.VMEM((16, cap // TILE // 4, TILE, LANES), jnp.bfloat16),
            pltpu.VMEM((4, 16, 128), jnp.float32),
            pltpu.VMEM((8, 16, 128), jnp.float32),
            pltpu.SemaphoreType.DMA((2,)),
            pltpu.SemaphoreType.DMA,
            pltpu.SemaphoreType.DMA((4,)),
            pltpu.SemaphoreType.DMA((4,)),
            pltpu.SemaphoreType.DMA((8,)),
            pltpu.SemaphoreType.DMA((8,)),
        ],
        compiler_params=pltpu.CompilerParams(
            collective_id=0, has_side_effects=True, vmem_limit_bytes=56 * 2**20
        ),
        name="move",
    )(lengths, moved_slot, hidden, queries, new_key, new_value, cache_keys, cache_values, w_out)

    chunks = 3
    cache_spec = pl.BlockSpec((1, cap // chunks, width), lambda c, s: (s, c, 0))
    keys_out, values_out = pl.pallas_call(
        place_kernel,
        grid=(chunks, slots),
        out_shape=(jax.ShapeDtypeStruct(cache_keys.shape, cache_keys.dtype),) * 2,
        in_specs=[
            smem_spec, smem_spec, vmem_spec, vmem_spec, cache_spec, cache_spec,
            pl.BlockSpec((16, cap // TILE // 4 // chunks, TILE, LANES), lambda c, s: (0, c, 0, 0)),
        ],
        out_specs=(cache_spec, cache_spec),
        compiler_params=pltpu.CompilerParams(vmem_limit_bytes=56 * 2**20),
        name="place",
    )(lengths, moved_slot, new_key, new_value, cache_keys, cache_values, arrived)
    return layer_out, keys_out, values_out


def solution(mesh):
    return jax.shard_map(
        shards,
        mesh=mesh,
        in_specs=(
            P("replica", None),
            P("replica", "tensor"),
            P("replica", "tensor"),
            P("replica", "tensor"),
            P("replica", None, "tensor"),
            P("replica", None, "tensor"),
            P("tensor", None),
            P(),
            P(),
        ),
        out_specs=(
            P("replica", "tensor"),
            P("replica", None, "tensor"),
            P("replica", None, "tensor"),
        ),
        check_vma=False,
    )
```

time: 171 us -> 89.1 us (0.52)
  waiting for transfers between devices: 123 us -> 0 us
  Pallas kernels: 0 us -> 86.5 us
  between operations: 16.1 us -> 0.65 us
  local copies, waits for them, and re-layouts: 9.6 us -> 0.6 us
  other arithmetic: 8.73 us -> 0 us
  starting transfers between devices: 6.79 us -> 0 us
  matrix products: 4.87 us -> 0 us
    pallas_call x0 -> x2, Pallas kernels: none -> 86.5 us  [the longest x1 80.3 us: shards(): pl.pallas_call(functools.partial(move_kernel, depth), out_shape=(jax.Shap...]
    ppermute x4 -> x0, waiting for transfers between devices: 63.4 us -> none  [swapped(): return lax.ppermute(block, axis, route)]
    unnamed x2 -> x0, waiting for transfers between devices: 59.6 us -> none
    ppermute x4 -> x0, starting transfers between devices: 6.75 us -> none  [swapped(): return lax.ppermute(block, axis, route)]
    select_n x4 -> x0, other arithmetic: 5.37 us -> none  [the longest x1 3.34 us: append_token(): jnp.where(positions < length_bound, cache, jnp.where(positions == length_...]
    dot_general x3 -> x0, matrix products: 4.87 us -> none  [the longest x1 2.85 us: head_terms(): lax.dot_general(w_out, attended, (((0,), (1,)), ((), ())), preferred_elem...]
    unnamed x8 -> x3, local copies, waits for them, and re-layouts: 5.07 us -> 0.6 us
    dynamic_slice x4 -> x0, local copies, waits for them, and re-layouts: 2.64 us -> none  [the longest x1 1.32 us: shards(): leaving_slot = moved_slot[replica_index]]
  transfers between devices with their start and end apart: 5 -> 0, of which waited for: 2 -> 0; matrix products, arithmetic and copies ran while one was open for 7% -> 0% of each run, Pallas kernels for 0% -> 0%
where the time goes in v1:
time: 89.1 us; the launch traced here: 87.8 us
  Pallas kernels  86.5 us (97%)
    pallas_call x1, Pallas kernels, shards(): pl.pallas_call(functools.partial(move_kernel, depth), out_shape=(jax.Shap...  80.3 us
    pallas_call x1, Pallas kernels, shards(): pl.pallas_call(place_kernel, grid=(chunks, slots), out_shape=(jax.ShapeDt...  6.28 us

profile of v1, /device:TPU:24, one launch (start us, length us, event | category | flops | bytes accessed | tf_op | source)
XLA Modules:
  0.0 87.8 jit_solution(9513416647252901067)
XLA Ops:
  0.6 80.3 %move.1 = (bf16[2,1024]{1,0:T(2,128)(2,1)}, bf16[16,12,16,256]{3,2,1,0:T(8,128)(2,1)}) custom-call(s32[128]{0:T(128)} %lengths.3, s32[64]{0:T(128)} %moved.3, bf16[2,4096]{1,0:T(2,128)(2,1)} %hidden.1, bf16[2,512]{1,0:T(2,128)(2,1)} %queries.1, bf16[2,512]{1,0:T(2,128)(2,1)} %new_key.3, bf16[2,512]{1,0:T(2,128)(2,1)} %new_value.3, ...), custom_call_target="tpu_custom_call" | custom-call | tf_op jit(solution)/shard_map/move/pallas_call | solution.py:208
  80.9 0.0 copy-start
  80.9 6.3 %place.1 = (bf16[2,768,512]{2,1,0:T(8,128)(2,1)}, bf16[2,768,512]{2,1,0:T(8,128)(2,1)}) custom-call(s32[128]{0:T(128)} %lengths.3, s32[64]{0:T(128)} %moved.3, bf16[2,512]{1,0:T(2,128)(2,1)} %new_key.3, bf16[2,512]{1,0:T(2,128)(2,1)} %new_value.3, bf16[2,768,512]{2,1,0:T(8,128)(2,1)} %cache_keys.3, bf16[2,768,512]{2,1,0:T(8,128)(2,1)} %cache_values.3, ...), custom_call_target="tpu_custom_call" | custom-call | tf_op jit(solution)/shard_map/place/pallas_call | solution.py:238
  87.2 0.0 copy-done
  87.2 0.6 copy.13
Async XLA Ops:
  80.9 6.3 %copy-start = (bf16[2,1024]{1,0:T(2,128)(2,1)S(1)}, bf16[2,1024]{1,0:T(2,128)(2,1)}, u32[]{:S(2)}) copy-start(bf16[2,1024]{1,0:T(2,128)(2,1)} %get-tuple-element.14) | copy-start | bytes 12292

commit v2 on v1

v2 whole, which is shorter than its diff:
```python
import functools

import jax
import jax.numpy as jnp
from jax import lax
from jax.experimental import pallas as pl
from jax.experimental.pallas import tpu as pltpu
from jax.sharding import PartitionSpec as P

HEAD_DIM = 128
TILE = 16
LANES = 256
MESH = pl.DeviceIdType.MESH

OFFSETS = ((0, 0), (1, 0), (3, 0), (0, 1), (0, 3), (1, 1), (3, 3), (1, 3), (3, 1), (2, 0), (0, 2))
K = len(OFFSETS)
SHORT = 36
CHUNKS = ((0, 4), (4, 8), (8, -(-SHORT * 4 // K)))
LEVELS = ((31, 25, 21), (39, 32, 29))
DIRECT_SHORT = ((0, 4), (4, 8), (8, -(-SHORT * 4 // K)))
DIRECT_WHOLE = ((0, 4), (4, 8), (8, 12), (12, 18))


def block_diagonal(row, heads):
    width = row.shape[1]
    row_id = lax.broadcasted_iota(jnp.int32, (8, width), 0)
    col_id = lax.broadcasted_iota(jnp.int32, (8, width), 1)
    own = (col_id >= row_id * HEAD_DIM) & (col_id < row_id * HEAD_DIM + HEAD_DIM)
    return own, jnp.where(own, jnp.broadcast_to(row, (8, width)), 0.0)


def attend_row(query, fresh_key, fresh_value, keys_ref, values_ref, length):
    width = keys_ref.shape[1]
    own, query_block = block_diagonal(query, width // HEAD_DIM)
    scale = HEAD_DIM**-0.5
    scores = lax.dot_general(
        query_block.astype(jnp.bfloat16), keys_ref[...], (((1,), (1,)), ((), ())), preferred_element_type=jnp.float32
    )
    scores = scores * scale
    fresh_score = jnp.sum(query_block * fresh_key, axis=1, keepdims=True) * scale
    position = lax.broadcasted_iota(jnp.int32, scores.shape, 1)
    live = position < length
    peak = jnp.maximum(jnp.max(jnp.where(live, scores, -1e30), axis=1, keepdims=True), fresh_score)
    terms = jnp.where(live, jnp.exp(jnp.minimum(scores - peak, 0.0)), 0.0)
    fresh_term = jnp.exp(fresh_score - peak)
    total = jnp.sum(terms, axis=1, keepdims=True) + fresh_term
    weights = (terms / total).astype(jnp.bfloat16)
    fresh_weight = (fresh_term / total).astype(jnp.bfloat16).astype(jnp.float32)
    mixed = lax.dot_general(
        weights, values_ref[...], (((1,), (0,)), ((), ())), preferred_element_type=jnp.float32
    )
    mixed = mixed + fresh_weight * fresh_value
    return jnp.sum(jnp.where(own, mixed, 0.0), axis=0, keepdims=True)


def as_rows(two_rows):
    count = two_rows.shape[1] // 128
    pieces = [two_rows[s : s + 1, j * 128 : (j + 1) * 128] for s in range(2) for j in range(count)]
    return jnp.concatenate(pieces, axis=0)


def as_line(rows):
    return jnp.concatenate([rows[j : j + 1, :] for j in range(rows.shape[0])], axis=1)


def replica_at(plane, x, y):
    return plane * 16 + (x % 4) * 4 + y % 4


def block_range(chunk, blocks):
    return chunk[0] * K // 4, min(blocks, chunk[1] * K // 4)


def move_kernel(
    chunks, slots, blocks,
    lengths, moved, hidden, queries, new_key, new_value, cache_keys, cache_values, w_out,
    small_out, arrived,
    keys, values, weights, partial, partial_in, fresh_out, fresh_in, landed,
    load_sem, part_send, part_recv, along_send, along_recv, out_send, out_recv, back_send, back_recv, store_sem,
    *buffers,
):
    spread = slots is not None
    count = len(chunks)
    outgoing, buffers = buffers[:count], buffers[count:]
    final, buffers = buffers[:count], buffers[count:]
    if spread:
        held, buffers = buffers[:count], buffers[count:]
        packed, buffers = buffers[:count], buffers[count:]
        unpacked, buffers = buffers[:count], buffers[count:]
        back = buffers
    replica = lax.axis_index("replica")
    tensor = lax.axis_index("tensor")
    plane, x, y = replica // 16, (replica // 4) % 4, replica % 4
    partner = (replica + 32) % 64

    loads = []
    for i, (source, target) in enumerate(((cache_keys, keys), (cache_values, values), (w_out, weights))):
        load = pltpu.make_async_copy(source, target, load_sem.at[i])
        load.start()
        loads.append(load)

    peers = [(replica, (tensor + k) % 4) for k in range(1, 4)]
    peers += [(partner, (tensor + k) % 4) for k in range(4)]
    if spread:
        peers += [(replica_at(plane, x + dx, y + dy), tensor) for dx, dy in OFFSETS[1:]]
    barrier = pltpu.get_barrier_semaphore()
    for peer in peers:
        pl.semaphore_signal(barrier, inc=1, device_id=peer, device_id_type=MESH)

    leaving = moved[replica]
    leaving_slot = jnp.maximum(leaving, 0)

    def items_of(source):
        slot = moved[source]
        length = lengths[source * 2 + jnp.maximum(slot, 0)]
        units = lax.div(length + TILE, TILE) * 4
        return jnp.where(slot >= 0, lax.div(units + (K - 1), K), 0)

    def send(source, target, device, send_sem, recv_sem):
        copy = pltpu.make_async_remote_copy(
            src_ref=source, dst_ref=target, send_sem=send_sem, recv_sem=recv_sem,
            device_id=device, device_id_type=MESH,
        )
        copy.start()
        return copy

    def copy_units(chunk, body):
        low, high = block_range(chunk, blocks)

        def step(block, carry):
            for quarter in range(4):
                unit = block * 4 + quarter
                body(block, quarter, unit % K, unit // K - chunk[0])
            return carry

        lax.fori_loop(low, high, step, 0)

    loads[0].wait()
    loads[1].wait()
    sent_out, sent_along, sent_back = [], [], []
    for c, chunk in enumerate(chunks):
        def pack(block, quarter, relay, item, c=c):
            held_rows = (keys, values)[quarter // 2]
            lanes = slice(quarter % 2 * LANES, (quarter % 2 + 1) * LANES)
            outgoing[c][relay, item] = held_rows[leaving_slot, pl.ds(block * TILE, TILE), lanes]

        copy_units(chunk, pack)
        if c == 0:
            pl.semaphore_wait(barrier, len(peers))
        if spread:
            sent = []
            for k in range(1, K):
                dx, dy = OFFSETS[k]
                sent.append(
                    send(
                        outgoing[c].at[k], held[c].at[k], (replica_at(plane, x + dx, y + dy), tensor),
                        out_send.at[c * K + k], out_recv.at[c * K + k],
                    )
                )
            sent_out.append(sent)

            def keep(item, carry, c=c):
                held[c][0, item] = outgoing[c][0, item]
                return carry

            lax.fori_loop(0, chunk[1] - chunk[0], keep, 0)
        else:
            sent_along.append(send(outgoing[c], final[c], (partner, tensor), along_send.at[c], along_recv.at[c]))

    def along(c):
        for copy in sent_out[c]:
            copy.wait_recv()
        low, high = chunks[c]
        counts, ends, total = [], [], 0
        for dx, dy in OFFSETS:
            live = jnp.clip(items_of(replica_at(plane, x - dx, y - dy)) - low, 0, high - low)
            total = total + live
            counts.append(live)
            ends.append(total)

        def step(slot, carry):
            source, base = 0, 0
            for live, end in zip(counts[:-1], ends[:-1]):
                past = slot >= end
                source = source + jnp.where(past, 1, 0)
                base = base + jnp.where(past, live, 0)
            packed[c][slot] = held[c][source, jnp.minimum(slot - base, high - low - 1)]
            return carry

        lax.fori_loop(0, slots[c], step, 0)
        sent_along.append(send(packed[c], unpacked[c], (partner, tensor), along_send.at[c], along_recv.at[c]))

    def spread_back(c):
        sent_along[c].wait_recv()
        low, high = chunks[c]
        starts, total = [], 0
        for dx, dy in OFFSETS:
            live = jnp.clip(items_of(replica_at((plane + 2) % 4, x - dx, y - dy)) - low, 0, high - low)
            starts.append(total)
            total = total + live

        def step(item, carry):
            for k in range(K):
                slot = jnp.minimum(starts[k] + item, slots[c] - 1)
                target = final if k == 0 else back
                target[c][k, item] = unpacked[c][slot]
            return carry

        lax.fori_loop(0, high - low, step, 0)
        sent = []
        for k in range(1, K):
            dx, dy = OFFSETS[k]
            sent.append(
                send(
                    back[c].at[k], final[c].at[k], (replica_at(plane, x - dx, y - dy), tensor),
                    back_send.at[c * K + k], back_recv.at[c * K + k],
                )
            )
        sent_back.append(sent)

    query_rows = queries[...].astype(jnp.float32)
    key_rows = new_key[...].astype(jnp.float32)
    value_rows = new_value[...].astype(jnp.float32)
    fresh_out[0:8] = as_rows(key_rows)
    fresh_out[8:16] = as_rows(value_rows)
    attended = []
    for slot in range(2):
        attended.append(
            attend_row(
                query_rows[slot : slot + 1], key_rows[slot : slot + 1], value_rows[slot : slot + 1],
                keys.at[slot], values.at[slot], lengths[replica * 2 + slot],
            )
        )
    attended = jnp.concatenate(attended + [jnp.zeros((6, attended[0].shape[1]), jnp.float32)], axis=0)
    attended = attended.astype(jnp.bfloat16)

    if spread:
        along(0)

    loads[2].wait()
    for piece in range(4):
        product = jnp.dot(
            attended, weights[:, piece * 1024 : (piece + 1) * 1024], preferred_element_type=jnp.float32
        )
        partial[piece] = as_rows(product[0:2])
    residual = hidden[:, pl.ds(pl.multiple_of(tensor * 1024, 1024), 1024)].astype(jnp.float32)
    partial[tensor] = partial[tensor] + as_rows(residual)

    shares = [send(fresh_out, fresh_in, (partner, tensor), part_send.at[0], part_recv.at[0])]
    for k in range(1, 8):
        piece = (tensor + k) % 4
        shares.append(
            send(
                partial.at[piece], partial_in.at[k], ((replica, partner)[k // 4], piece),
                part_send.at[k], part_recv.at[k],
            )
        )

    if spread:
        along(1)
        spread_back(0)
        along(2)

    for share in shares:
        share.wait()
    here = partial[tensor] + partial_in[1] + partial_in[2] + partial_in[3]
    there = partial_in[4] + partial_in[5] + partial_in[6] + partial_in[7]
    coming = jnp.where(moved[partner] == 1, there[8:16], there[0:8])
    for slot in range(2):
        small_out[slot * 8 : slot * 8 + 8] = jnp.where(leaving == slot, coming, here[slot * 8 : slot * 8 + 8])
    small_out[16:32] = fresh_in[...]

    if spread:
        spread_back(1)

    stores = []
    for c, chunk in enumerate(chunks):
        if spread:
            if c == count - 1:
                spread_back(c)
            for copy in sent_back[c]:
                copy.wait_recv()
        else:
            sent_along[c].wait_recv()

        def unpack(block, quarter, relay, item, c=c):
            lanes = slice(quarter % 2 * LANES, (quarter % 2 + 1) * LANES)
            landed[quarter // 2, pl.ds(block * TILE, TILE), lanes] = final[c][relay, item]

        copy_units(chunk, unpack)
        low, high = block_range(chunk, blocks)
        for kind in range(2):
            span = slice(low * TILE, high * TILE)
            store = pltpu.make_async_copy(
                landed.at[kind, span], arrived.at[kind, span], store_sem.at[c * 2 + kind]
            )
            store.start()
            stores.append(store)
    for sent in sent_out + [sent_along] + sent_back:
        for copy in sent:
            copy.wait_send()
    for store in stores:
        store.wait()


def move(chunks, slots, blocks, collective_id, *operands):
    cache_keys, w_out = operands[6], operands[8]
    here, cap, width = cache_keys.shape
    count = len(chunks)
    any_spec = pl.BlockSpec(memory_space=pl.ANY)
    vmem_spec = pl.BlockSpec(memory_space=pltpu.VMEM)
    smem_spec = pl.BlockSpec(memory_space=pltpu.SMEM)

    def items(kind=1):
        return [pltpu.VMEM((K, high - low, TILE, LANES), jnp.bfloat16) for low, high in chunks]

    buffers = items() + items()
    if slots is not None:
        on_the_way = [pltpu.VMEM((size, TILE, LANES), jnp.bfloat16) for size in slots]
        buffers += items() + on_the_way + on_the_way + items()
    return pl.pallas_call(
        functools.partial(move_kernel, chunks, slots, blocks),
        out_shape=(
            jax.ShapeDtypeStruct((32, 128), jnp.float32),
            jax.ShapeDtypeStruct((2, cap, width), jnp.bfloat16),
        ),
        in_specs=[smem_spec] * 2 + [vmem_spec] * 4 + [any_spec] * 3,
        out_specs=(vmem_spec, any_spec),
        scratch_shapes=[
            pltpu.VMEM((here, cap, width), jnp.bfloat16),
            pltpu.VMEM((here, cap, width), jnp.bfloat16),
            pltpu.VMEM(w_out.shape, jnp.bfloat16),
            pltpu.VMEM((4, 16, 128), jnp.float32),
            pltpu.VMEM((8, 16, 128), jnp.float32),
            pltpu.VMEM((16, 128), jnp.float32),
            pltpu.VMEM((16, 128), jnp.float32),
            pltpu.VMEM((2, cap, width), jnp.bfloat16),
            pltpu.SemaphoreType.DMA((3,)),
            pltpu.SemaphoreType.DMA((8,)),
            pltpu.SemaphoreType.DMA((8,)),
            pltpu.SemaphoreType.DMA((count,)),
            pltpu.SemaphoreType.DMA((count,)),
            pltpu.SemaphoreType.DMA((count * K,)),
            pltpu.SemaphoreType.DMA((count * K,)),
            pltpu.SemaphoreType.DMA((count * K,)),
            pltpu.SemaphoreType.DMA((count * K,)),
            pltpu.SemaphoreType.DMA((2 * count,)),
            *buffers,
        ],
        compiler_params=pltpu.CompilerParams(
            collective_id=collective_id, has_side_effects=True, vmem_limit_bytes=56 * 2**20
        ),
        name="move%d" % collective_id,
    )(*operands)


def place_kernel(
    lengths, moved, new_key, new_value, small, cache_keys, cache_values, arrived,
    layer_out, keys_out, values_out,
    rows, read_sem, write_sem,
):
    replica = lax.axis_index("replica")
    partner = (replica + 32) % 64
    arriving_length = lengths[partner * 2 + jnp.maximum(moved[partner], 0)]
    arriving_slot = moved[partner]
    sources, targets = (cache_keys, cache_values), (keys_out, values_out)
    jobs = [(slot, kind) for slot in range(2) for kind in range(2)]
    for slot, kind in jobs:
        comes = moved[replica] == slot

        @pl.when(comes)
        def _(slot=slot, kind=kind):
            pltpu.make_async_copy(arrived.at[kind], rows.at[slot, kind], read_sem.at[slot * 2 + kind]).start()

        @pl.when(jnp.logical_not(comes))
        def _(slot=slot, kind=kind):
            pltpu.make_async_copy(sources[kind].at[slot], rows.at[slot, kind], read_sem.at[slot * 2 + kind]).start()

    layer_out[...] = jnp.concatenate([as_line(small[0:8]), as_line(small[8:16])], axis=0).astype(jnp.bfloat16)
    cap, width = rows.shape[2:]
    in_tile = lax.broadcasted_iota(jnp.int32, (TILE, width), 0)
    writes = []
    for slot, kind in jobs:
        comes = moved[replica] == slot
        length = jnp.where(comes, arriving_length, lengths[replica * 2 + slot])
        own_fresh = (new_key, new_value)[kind][...].astype(jnp.float32)[slot : slot + 1]
        come_fresh = small[16 + kind * 8 : 24 + kind * 8]
        come_fresh = as_line(jnp.where(arriving_slot == 1, come_fresh[4:8], come_fresh[0:4]))
        fresh = jnp.broadcast_to(jnp.where(comes, come_fresh, own_fresh), (TILE, width))
        pltpu.make_async_copy(sources[kind].at[slot], rows.at[slot, kind], read_sem.at[slot * 2 + kind]).wait()
        last = lax.div(length, TILE)
        span = pl.ds(pl.multiple_of(last * TILE, TILE), TILE)
        position = in_tile + last * TILE
        edge = rows[slot, kind, span, :].astype(jnp.float32)
        edge = jnp.where(position < length, edge, jnp.where(position == length, fresh, 0.0))
        rows[slot, kind, span, :] = edge.astype(jnp.bfloat16)

        def clear(block, carry, slot=slot, kind=kind):
            dead = pl.ds(pl.multiple_of(block * TILE, TILE), TILE)
            rows[slot, kind, dead, :] = jnp.zeros((TILE, width), jnp.bfloat16)
            return carry

        lax.fori_loop(last + 1, cap // TILE, clear, 0)
        write = pltpu.make_async_copy(rows.at[slot, kind], targets[kind].at[slot], write_sem.at[slot * 2 + kind])
        write.start()
        writes.append(write)
    for write in writes:
        write.wait()


def choose_kernel(lengths, moved, choice):
    row = lax.broadcasted_iota(jnp.int32, (64, 64), 0)
    col = lax.broadcasted_iota(jnp.int32, (64, 64), 1)
    slot = jnp.sum(jnp.where(row == col, moved[...].astype(jnp.float32), 0.0), axis=1, keepdims=True)
    moves = slot >= 0.0
    wide_row = lax.broadcasted_iota(jnp.int32, (64, 128), 0)
    wide_col = lax.broadcasted_iota(jnp.int32, (64, 128), 1)
    wanted = wide_col.astype(jnp.float32) == 2.0 * wide_row.astype(jnp.float32) + jnp.maximum(slot, 0.0)
    length = jnp.sum(jnp.where(wanted, lengths[...].astype(jnp.float32), 0.0), axis=1, keepdims=True)
    blocks = jnp.where(moves, jnp.floor((length + TILE) * (1.0 / TILE)), 0.0)
    items = jnp.floor((blocks * 4.0 + (K - 0.5)) * (1.0 / K))
    longest = jnp.max(blocks).astype(jnp.int32)
    relays = row < 0
    for dx, dy in OFFSETS:
        there = (row & 48) + ((((row >> 2) + dx) & 3) << 2) + ((row + dy) & 3)
        relays = relays | (there == col)
    needs = []
    for low, high in CHUNKS:
        live = jnp.clip(items - low, 0.0, float(high - low))
        needs.append(jnp.max(jnp.sum(jnp.where(relays, live, 0.0), axis=0)).astype(jnp.int32))
    result = 0
    for level in LEVELS:
        fits = longest <= SHORT
        for need, size in zip(needs, level):
            fits = fits & (need <= size)
        result = result + jnp.where(fits, 0, 1)
    choice[0] = result + jnp.where(longest <= SHORT, 0, 1)


def shards(
    hidden, queries, new_key, new_value, cache_keys, cache_values, w_out, lengths, moved_slot
):
    slots, cap, width = cache_keys.shape
    any_spec = pl.BlockSpec(memory_space=pl.ANY)
    vmem_spec = pl.BlockSpec(memory_space=pltpu.VMEM)
    smem_spec = pl.BlockSpec(memory_space=pltpu.SMEM)

    choice = pl.pallas_call(
        choose_kernel,
        out_shape=jax.ShapeDtypeStruct((1,), jnp.int32),
        in_specs=[vmem_spec] * 2,
        out_specs=smem_spec,
        name="choose",
    )(lengths.reshape(1, -1), moved_slot.reshape(1, -1))

    builds = [functools.partial(move, CHUNKS, level, SHORT, i) for i, level in enumerate(LEVELS)]
    builds.append(functools.partial(move, DIRECT_SHORT, None, SHORT, len(builds)))
    builds.append(functools.partial(move, DIRECT_WHOLE, None, cap // TILE, len(builds)))
    small, arrived = lax.switch(
        choice[0], builds,
        lengths, moved_slot, hidden, queries, new_key, new_value, cache_keys, cache_values, w_out,
    )

    return pl.pallas_call(
        place_kernel,
        out_shape=(
            jax.ShapeDtypeStruct((slots, w_out.shape[1] // 4), jnp.bfloat16),
            jax.ShapeDtypeStruct(cache_keys.shape, cache_keys.dtype),
            jax.ShapeDtypeStruct(cache_keys.shape, cache_keys.dtype),
        ),
        in_specs=[smem_spec] * 2 + [vmem_spec] * 3 + [any_spec] * 3,
        out_specs=(vmem_spec, any_spec, any_spec),
        scratch_shapes=[
            pltpu.VMEM((slots, 2, cap, width), jnp.bfloat16),
            pltpu.SemaphoreType.DMA((4,)),
            pltpu.SemaphoreType.DMA((4,)),
        ],
        compiler_params=pltpu.CompilerParams(vmem_limit_bytes=56 * 2**20),
        name="place",
    )(lengths, moved_slot, new_key, new_value, small, cache_keys, cache_values, arrived)


def solution(mesh):
    return jax.shard_map(
        shards,
        mesh=mesh,
        in_specs=(
            P("replica", None),
            P("replica", "tensor"),
            P("replica", "tensor"),
            P("replica", "tensor"),
            P("replica", None, "tensor"),
            P("replica", None, "tensor"),
            P("tensor", None),
            P(),
            P(),
        ),
        out_specs=(
            P("replica", "tensor"),
            P("replica", None, "tensor"),
            P("replica", None, "tensor"),
        ),
        check_vma=False,
    )
```

time: 89.1 us -> 66.4 us (0.75); the launches traced: 87.8 us -> 66.2 us
  Pallas kernels: 86.5 us -> 64.9 us
    pallas_call x2 -> x3, Pallas kernels: 86.5 us -> 64.9 us  [the longest x1 59 us: move(): pl.pallas_call(functools.partial(move_kernel, chunks, slots, blocks), out...]
where the time goes in v2:
time: 66.4 us; the launch traced here: 66.2 us
  Pallas kernels  64.9 us (98%)
  between operations  1.29 us (2%)
    pallas_call x1, Pallas kernels, move(): pl.pallas_call(functools.partial(move_kernel, chunks, slots, blocks), out...  59 us
    pallas_call x1, Pallas kernels, shards(): pl.pallas_call(place_kernel, out_shape=(jax.ShapeDtypeStruct((slots, w_ou...  4.4 us
    pallas_call x1, Pallas kernels, shards(): pl.pallas_call(choose_kernel, out_shape=jax.ShapeDtypeStruct((1,), jnp.in...  1.51 us

profile of v2, /device:TPU:24, one launch (start us, length us, event | category | flops | bytes accessed | tf_op | source)
XLA Modules:
  0.0 66.2 jit_solution(6767225872279741096)
XLA Ops:
  0.6 1.5 %choose.1 = s32[1]{0:T(128)} custom-call(s32[1,128]{1,0:T(1,128)} %bitcast.3, s32[1,64]{1,0:T(1,128)} %bitcast.4), custom_call_target="tpu_custom_call" | custom-call | tf_op jit(solution)/shard_map/choose/pallas_call | solution.py:448
  2.8 59.0 %conditional.1 = ((f32[32,128]{1,0:T(8,128)S(1)}, bf16[2,768,512]{2,1,0:T(8,128)(2,1)S(1)})) conditional(s32[]{:T(128)} %bitcast.2, (s32[128]{0:T(128)}, s32[64]{0:T(128)}, bf16[2,4096]{1,0:T(2,128)(2,1)}, bf16[2,512]{1,0:T(2,128)(2,1)}, bf16[2,512]{1,0:T(2,128)(2,1)}, /*index=5*/bf16[2,512]{1,0:T(2,128)(2,1)}, ...), branch_computations={%region_0.0_spmd, %region_1.0_spmd, %region_2.0_spmd, %region_3.0_... | conditional | bytes 8 | solution.py:459
  2.8 59.0 %move0.1 = (f32[32,128]{1,0:T(8,128)S(1)}, bf16[2,768,512]{2,1,0:T(8,128)(2,1)S(1)}) custom-call(s32[128]{0:T(128)} %get-tuple-element.72.lengths, s32[64]{0:T(128)} %get-tuple-element.73.moved, bf16[2,4096]{1,0:T(2,128)(2,1)} %get-tuple-element.74.hidden, bf16[2,512]{1,0:T(2,128)(2,1)} %get-tuple-element.75.queries, ...), custom_call_target="tpu_custom_call" | custom-call | tf_op jit(solution)/shard_map/cond/branch_0_fun/move0/pallas_call | solution.py:321
  61.8 4.4 %place.1 = (bf16[2,1024]{1,0:T(2,128)(2,1)}, bf16[2,768,512]{2,1,0:T(8,128)(2,1)}, bf16[2,768,512]{2,1,0:T(8,128)(2,1)}) custom-call(s32[128]{0:T(128)} %lengths.1, s32[64]{0:T(128)} %moved.1, bf16[2,512]{1,0:T(2,128)(2,1)} %new_key.1, bf16[2,512]{1,0:T(2,128)(2,1)} %new_value.1, f32[32,128]{1,0:T(8,128)S(1)} %get-tuple-element.113.small, ...), custom_call_target="tpu_custom_call" | custom-call | tf_op jit(solution)/shard_map/place/pallas_call | solution.py:464

commit v3 on v2

v3 whole, which is shorter than its diff:
```python
import functools

import jax
import jax.numpy as jnp
from jax import lax
from jax.experimental import pallas as pl
from jax.experimental.pallas import tpu as pltpu
from jax.sharding import PartitionSpec as P

HEAD_DIM = 128
TILE = 16
LANES = 256
MESH = pl.DeviceIdType.MESH

OFFSETS = tuple((dx, dy) for dx in range(4) for dy in range(4))
K = len(OFFSETS)
STEP = K // 4
SHORT = 36
CHUNKS = ((0, 1), (1, 4), (4, 6), (6, 9))
LEVELS = ((0, 21, 12, 12), (0, 26, 14, 16), (0, 31, 18, 19))
DIRECT = (0, 0, 0, 0)
WHOLE = ((0, 3), (3, 6), (6, 9), (9, 12))
PART = 128
SPLIT = 256


def block_diagonal(row, heads):
    width = row.shape[1]
    row_id = lax.broadcasted_iota(jnp.int32, (8, width), 0)
    col_id = lax.broadcasted_iota(jnp.int32, (8, width), 1)
    own = (col_id >= row_id * HEAD_DIM) & (col_id < row_id * HEAD_DIM + HEAD_DIM)
    return own, jnp.where(own, jnp.broadcast_to(row, (8, width)), 0.0)


def attend_row(query, fresh_key, fresh_value, keys_ref, values_ref, length):
    width = keys_ref.shape[1]
    own, query_block = block_diagonal(query, width // HEAD_DIM)
    scale = HEAD_DIM**-0.5
    scores = lax.dot_general(
        query_block.astype(jnp.bfloat16), keys_ref[...], (((1,), (1,)), ((), ())), preferred_element_type=jnp.float32
    )
    scores = scores * scale
    fresh_score = jnp.sum(query_block * fresh_key, axis=1, keepdims=True) * scale
    position = lax.broadcasted_iota(jnp.int32, scores.shape, 1)
    live = position < length
    peak = jnp.maximum(jnp.max(jnp.where(live, scores, -1e30), axis=1, keepdims=True), fresh_score)
    terms = jnp.where(live, jnp.exp(jnp.minimum(scores - peak, 0.0)), 0.0)
    fresh_term = jnp.exp(fresh_score - peak)
    total = jnp.sum(terms, axis=1, keepdims=True) + fresh_term
    weights = (terms / total).astype(jnp.bfloat16)
    fresh_weight = (fresh_term / total).astype(jnp.bfloat16).astype(jnp.float32)
    mixed = lax.dot_general(
        weights, values_ref[...], (((1,), (0,)), ((), ())), preferred_element_type=jnp.float32
    )
    mixed = mixed + fresh_weight * fresh_value
    return jnp.sum(jnp.where(own, mixed, 0.0), axis=0, keepdims=True)


def as_rows(two_rows):
    count = two_rows.shape[1] // 128
    pieces = [two_rows[s : s + 1, j * 128 : (j + 1) * 128] for s in range(2) for j in range(count)]
    return jnp.concatenate(pieces, axis=0)


def as_line(rows):
    return jnp.concatenate([rows[j : j + 1, :] for j in range(rows.shape[0])], axis=1)


def replica_at(plane, x, y):
    return plane * 16 + (x % 4) * 4 + y % 4


def items_in(blocks):
    return (blocks + (STEP - 1)) * (128 // STEP + 1) >> 7 if STEP == 3 else (blocks + (STEP - 1)) >> (STEP.bit_length() - 1)


def move_kernel(
    chunks, slots,
    lengths, moved, hidden, queries, new_key, new_value, cache_keys, cache_values, w_out,
    small_out, arrived,
    keys, values, weights, partial, partial_in, fresh_out, fresh_in, landed,
    load_sem, part_send, part_recv, along_send, along_recv, out_send, out_recv, back_send, back_recv, store_sem,
    *buffers,
):
    count = len(chunks)
    outgoing, buffers = buffers[:count], buffers[count:]
    final, buffers = buffers[:count], buffers[count:]
    held, packed, unpacked, back = {}, {}, {}, {}
    spread = [c for c in range(count) if slots[c]]
    for i, c in enumerate(spread):
        held[c], packed[c], unpacked[c], back[c] = buffers[i * 4 : i * 4 + 4]
    replica = lax.axis_index("replica")
    tensor = lax.axis_index("tensor")
    plane, x, y = replica // 16, (replica // 4) % 4, replica % 4
    partner = (replica + 32) % 64

    loads = []
    parts = [(cache, held_rows, span) for span in (slice(0, SPLIT), slice(SPLIT, None)) for cache, held_rows in ((cache_keys, keys), (cache_values, values))]
    for i, (cache, held_rows, span) in enumerate(parts):
        loads.append(pltpu.make_async_copy(cache.at[:, span], held_rows.at[:, span], load_sem.at[i]))
    loads.append(pltpu.make_async_copy(w_out, weights, load_sem.at[4]))
    for load in loads:
        load.start()

    peers = [(replica, (tensor + k) % 4) for k in range(1, 4)]
    peers += [(partner, (tensor + k) % 4) for k in range(4)]
    if spread:
        peers += [(replica_at(plane, x + dx, y + dy), tensor) for dx, dy in OFFSETS[1:]]
    barrier = pltpu.get_barrier_semaphore()
    for peer in peers:
        pl.semaphore_signal(barrier, inc=1, device_id=peer, device_id_type=MESH)

    leaving = moved[replica]

    def items_of(source):
        slot = moved[source]
        length = lengths[source * 2 + jnp.maximum(slot, 0)]
        return jnp.where(slot >= 0, items_in((length + TILE) >> 4), 0)

    def send(source, target, device, send_sem, recv_sem):
        copy = pltpu.make_async_remote_copy(
            src_ref=source, dst_ref=target, send_sem=send_sem, recv_sem=recv_sem,
            device_id=device, device_id_type=MESH,
        )
        copy.start()
        return copy

    def copy_units(chunk, body):
        def step(item, carry):
            for k in range(K):
                rows = pl.ds(pl.multiple_of((item * STEP + k // 4) * TILE, TILE), TILE)
                lanes = slice(k % 2 * LANES, (k % 2 + 1) * LANES)
                body(k % 4 // 2, rows, lanes, k, item - chunk[0])
            return carry

        lax.fori_loop(chunk[0], chunk[1], step, 0)

    waited = 0
    sent_out, sent_along, sent_back = {}, {}, {}
    for c, chunk in enumerate(chunks):
        if c == 0 or (waited == 2 and chunk[1] * STEP * TILE > SPLIT):
            loads[waited].wait()
            loads[waited + 1].wait()
            waited += 2
            if chunk[1] * STEP * TILE > SPLIT and waited == 2:
                loads[2].wait()
                loads[3].wait()
                waited = 4

        def pack(kind, rows, lanes, relay, item, c=c):
            held_rows = (keys, values)[kind]
            outgoing[c][relay, item] = jnp.where(leaving == 1, held_rows[1, rows, lanes], held_rows[0, rows, lanes])

        copy_units(chunk, pack)
        if c == 0:
            pl.semaphore_wait(barrier, len(peers))
        if not slots[c]:
            sent_along[c] = send(outgoing[c], final[c], (partner, tensor), along_send.at[c], along_recv.at[c])
            continue
        sent_out[c] = []
        for k in range(1, K):
            dx, dy = OFFSETS[k]
            sent_out[c].append(
                send(
                    outgoing[c].at[k], held[c].at[k], (replica_at(plane, x + dx, y + dy), tensor),
                    out_send.at[c * K + k], out_recv.at[c * K + k],
                )
            )

        def keep(item, carry, c=c):
            held[c][0, item] = outgoing[c][0, item]
            return carry

        lax.fori_loop(0, chunk[1] - chunk[0], keep, 0)
    if waited == 2:
        loads[2].wait()
        loads[3].wait()

    if spread:
        leave_items = [items_of(replica_at(plane, x - dx, y - dy)) for dx, dy in OFFSETS]
        come_items = [items_of(replica_at((plane + 2) % 4, x - dx, y - dy)) for dx, dy in OFFSETS]

    def along(c):
        for copy in sent_out[c]:
            copy.wait_recv()
        low, high = chunks[c]
        counts, ends, total = [], [], 0
        for items in leave_items:
            live = jnp.clip(items - low, 0, high - low)
            total = total + live
            counts.append(live)
            ends.append(total)

        def step(slot, carry):
            source, base = 0, 0
            for live, end in zip(counts[:-1], ends[:-1]):
                past = slot >= end
                source = source + jnp.where(past, 1, 0)
                base = base + jnp.where(past, live, 0)
            item = jnp.minimum(slot - base, high - low - 1)
            packed[c][slot] = held[c][source, item]
            return carry

        lax.fori_loop(0, slots[c], step, 0)
        sent_along[c] = send(packed[c], unpacked[c], (partner, tensor), along_send.at[c], along_recv.at[c])

    def spread_back(c):
        sent_along[c].wait_recv()
        low, high = chunks[c]
        starts, total = [], 0
        for items in come_items:
            starts.append(total)
            total = total + jnp.clip(items - low, 0, high - low)
        sent_back[c] = []
        for k in range(K - 1, -1, -1):
            target = final[c] if k == 0 else back[c]
            for item in range(high - low):
                target[k, item] = unpacked[c][jnp.minimum(starts[k] + item, slots[c] - 1)]
            if k:
                dx, dy = OFFSETS[k]
                sent_back[c].append(
                    send(
                        back[c].at[k], final[c].at[k], (replica_at(plane, x - dx, y - dy), tensor),
                        back_send.at[c * K + k], back_recv.at[c * K + k],
                    )
                )

    query_rows = queries[...].astype(jnp.float32)
    key_rows = new_key[...].astype(jnp.float32)
    value_rows = new_value[...].astype(jnp.float32)
    fresh_out[0:8] = as_rows(key_rows)
    fresh_out[8:16] = as_rows(value_rows)
    attended = []
    for slot in range(2):
        attended.append(
            attend_row(
                query_rows[slot : slot + 1], key_rows[slot : slot + 1], value_rows[slot : slot + 1],
                keys.at[slot], values.at[slot], lengths[replica * 2 + slot],
            )
        )
    attended = jnp.concatenate(attended + [jnp.zeros((6, attended[0].shape[1]), jnp.float32)], axis=0)
    attended = attended.astype(jnp.bfloat16)

    loads[4].wait()
    for piece in range(4):
        product = jnp.dot(
            attended, weights[:, piece * 1024 : (piece + 1) * 1024], preferred_element_type=jnp.float32
        )
        partial[piece] = as_rows(product[0:2])
    residual = hidden[:, pl.ds(pl.multiple_of(tensor * 1024, 1024), 1024)].astype(jnp.float32)
    partial[tensor] = partial[tensor] + as_rows(residual)

    shares = [send(fresh_out, fresh_in, (partner, tensor), part_send.at[0], part_recv.at[0])]
    for k in range(1, 8):
        piece = (tensor + k) % 4
        shares.append(
            send(
                partial.at[piece], partial_in.at[k], ((replica, partner)[k // 4], piece),
                part_send.at[k], part_recv.at[k],
            )
        )

    for c in spread:
        along(c)
        spread_back(c)

    for share in shares:
        share.wait()
    here = partial[tensor] + partial_in[1] + partial_in[2] + partial_in[3]
    there = partial_in[4] + partial_in[5] + partial_in[6] + partial_in[7]
    coming = jnp.where(moved[partner] == 1, there[8:16], there[0:8])
    for slot in range(2):
        small_out[slot * 8 : slot * 8 + 8] = jnp.where(leaving == slot, coming, here[slot * 8 : slot * 8 + 8])
    small_out[16:32] = fresh_in[...]

    stores = []
    for c, chunk in enumerate(chunks):
        if not slots[c]:
            sent_along[c].wait_recv()
        else:
            for copy in sent_back[c]:
                copy.wait_recv()

        def unpack(kind, rows, lanes, relay, item, c=c):
            landed[kind, rows, lanes] = final[c][relay, item]

        copy_units(chunk, unpack)
        for kind in range(2):
            span = slice(chunk[0] * STEP * TILE, chunk[1] * STEP * TILE)
            store = pltpu.make_async_copy(
                landed.at[kind, span], arrived.at[kind, span], store_sem.at[c * 2 + kind]
            )
            store.start()
            stores.append(store)
    for copy in sent_along.values():
        copy.wait_send()
    for sent in (sent_out, sent_back):
        for copies in sent.values():
            for copy in copies:
                copy.wait_send()
    for store in stores:
        store.wait()


def move(chunks, slots, collective_id, *operands):
    cache_keys, w_out = operands[6], operands[8]
    here, cap, width = cache_keys.shape
    count = len(chunks)
    any_spec = pl.BlockSpec(memory_space=pl.ANY)
    vmem_spec = pl.BlockSpec(memory_space=pltpu.VMEM)
    smem_spec = pl.BlockSpec(memory_space=pltpu.SMEM)

    def items(chunk):
        return pltpu.VMEM((K, chunk[1] - chunk[0], TILE, LANES), jnp.bfloat16)

    buffers = [items(chunk) for chunk in chunks] * 2
    for chunk, size in zip(chunks, slots):
        if size:
            on_the_way = pltpu.VMEM((size, TILE, LANES), jnp.bfloat16)
            buffers += [items(chunk), on_the_way, on_the_way, items(chunk)]
    return pl.pallas_call(
        functools.partial(move_kernel, chunks, slots),
        out_shape=(
            jax.ShapeDtypeStruct((32, 128), jnp.float32),
            jax.ShapeDtypeStruct((2, cap, width), jnp.bfloat16),
        ),
        in_specs=[smem_spec] * 2 + [vmem_spec] * 4 + [any_spec] * 3,
        out_specs=(vmem_spec, any_spec),
        scratch_shapes=[
            pltpu.VMEM((here, cap, width), jnp.bfloat16),
            pltpu.VMEM((here, cap, width), jnp.bfloat16),
            pltpu.VMEM(w_out.shape, jnp.bfloat16),
            pltpu.VMEM((4, 16, 128), jnp.float32),
            pltpu.VMEM((8, 16, 128), jnp.float32),
            pltpu.VMEM((16, 128), jnp.float32),
            pltpu.VMEM((16, 128), jnp.float32),
            pltpu.VMEM((2, cap, width), jnp.bfloat16),
            pltpu.SemaphoreType.DMA((5,)),
            pltpu.SemaphoreType.DMA((8,)),
            pltpu.SemaphoreType.DMA((8,)),
            pltpu.SemaphoreType.DMA((count,)),
            pltpu.SemaphoreType.DMA((count,)),
            pltpu.SemaphoreType.DMA((count * K,)),
            pltpu.SemaphoreType.DMA((count * K,)),
            pltpu.SemaphoreType.DMA((count * K,)),
            pltpu.SemaphoreType.DMA((count * K,)),
            pltpu.SemaphoreType.DMA((2 * count,)),
            *buffers,
        ],
        compiler_params=pltpu.CompilerParams(
            collective_id=collective_id, has_side_effects=True, vmem_limit_bytes=56 * 2**20
        ),
        name="move%d" % collective_id,
    )(*operands)


def place_kernel(
    lengths, moved, new_key, new_value, small, cache_keys, cache_values, arrived,
    layer_out, keys_out, values_out,
    zeros, rows, read_sem, write_sem,
):
    replica = lax.axis_index("replica")
    partner = (replica + 32) % 64
    arriving_length = lengths[partner * 2 + jnp.maximum(moved[partner], 0)]
    arriving_slot = moved[partner]
    cap, width = keys_out.shape[1:]
    spans = cap // PART
    jobs = []
    for slot in range(2):
        comes = moved[replica] == slot
        length = jnp.where(comes, arriving_length, lengths[replica * 2 + slot])
        last = lax.shift_right_logical(length, PART.bit_length() - 1)
        for kind, (cache, target) in enumerate(((cache_keys, keys_out), (cache_values, values_out))):
            for part in range(spans):
                span = slice(part * PART, (part + 1) * PART)
                sem = read_sem.at[(slot * 2 + kind) * spans + part]

                @pl.when((part <= last) & comes)
                def _(slot=slot, kind=kind, span=span, sem=sem):
                    pltpu.make_async_copy(arrived.at[kind, span], rows.at[slot, kind, span], sem).start()

                @pl.when((part <= last) & jnp.logical_not(comes))
                def _(slot=slot, kind=kind, span=span, sem=sem, cache=cache):
                    pltpu.make_async_copy(cache.at[slot, span], rows.at[slot, kind, span], sem).start()

            jobs.append((slot, kind, comes, length, last, cache.at[slot], target.at[slot]))
    zeros[...] = jnp.zeros_like(zeros)
    for slot, kind, comes, length, last, cache, target in jobs:
        for part in range(spans):
            span = slice(part * PART, (part + 1) * PART)

            @pl.when(part > last)
            def _(slot=slot, kind=kind, target=target, span=span, part=part):
                sem = write_sem.at[(slot * 2 + kind) * spans + part]
                pltpu.make_async_copy(zeros, target.at[span], sem).start()

    layer_out[...] = jnp.concatenate([as_line(small[0:8]), as_line(small[8:16])], axis=0).astype(jnp.bfloat16)
    in_part = lax.broadcasted_iota(jnp.int32, (PART, width), 0)
    for slot, kind, comes, length, last, cache, target in jobs:
        own_fresh = (new_key, new_value)[kind][...].astype(jnp.float32)[slot : slot + 1]
        come_fresh = small[16 + kind * 8 : 24 + kind * 8]
        come_fresh = as_line(jnp.where(arriving_slot == 1, come_fresh[4:8], come_fresh[0:4]))
        fresh = jnp.broadcast_to(jnp.where(comes, come_fresh, own_fresh), (PART, width))
        for part in range(spans):
            span = slice(part * PART, (part + 1) * PART)

            @pl.when(part <= last)
            def _(slot=slot, kind=kind, cache=cache, target=target, span=span, part=part):
                index = (slot * 2 + kind) * spans + part
                pltpu.make_async_copy(cache.at[span], rows.at[slot, kind, span], read_sem.at[index]).wait()

                @pl.when(part == last)
                def _():
                    position = in_part + part * PART
                    edge = rows[slot, kind, span].astype(jnp.float32)
                    edge = jnp.where(position < length, edge, jnp.where(position == length, fresh, 0.0))
                    rows[slot, kind, span] = edge.astype(jnp.bfloat16)

                pltpu.make_async_copy(rows.at[slot, kind, span], target.at[span], write_sem.at[index]).start()
    for slot, kind, comes, length, last, cache, target in jobs:
        for part in range(spans):
            span = slice(part * PART, (part + 1) * PART)
            sem = write_sem.at[(slot * 2 + kind) * spans + part]
            pltpu.make_async_copy(zeros, target.at[span], sem).wait()


def choose_kernel(lengths, moved, choice):
    row = lax.broadcasted_iota(jnp.int32, (64, 64), 0)
    col = lax.broadcasted_iota(jnp.int32, (64, 64), 1)
    slot = jnp.sum(jnp.where(row == col, moved[...].astype(jnp.float32), 0.0), axis=1, keepdims=True)
    moves = slot >= 0.0
    wide_row = lax.broadcasted_iota(jnp.int32, (64, 128), 0)
    wide_col = lax.broadcasted_iota(jnp.int32, (64, 128), 1)
    wanted = wide_col.astype(jnp.float32) == 2.0 * wide_row.astype(jnp.float32) + jnp.maximum(slot, 0.0)
    length = jnp.sum(jnp.where(wanted, lengths[...].astype(jnp.float32), 0.0), axis=1, keepdims=True)
    blocks = jnp.where(moves, jnp.floor((length + TILE) * (1.0 / TILE)), 0.0)
    items = jnp.floor((blocks + (STEP - 0.5)) * (1.0 / STEP))
    longest = jnp.max(blocks).astype(jnp.int32)
    relays = row < 0
    for dx, dy in OFFSETS:
        there = (row & 48) + ((((row >> 2) + dx) & 3) << 2) + ((row + dy) & 3)
        relays = relays | (there == col)
    needs = []
    for low, high in CHUNKS[1:]:
        live = jnp.clip(items - low, 0.0, float(high - low))
        needs.append(jnp.max(jnp.sum(jnp.where(relays, live, 0.0), axis=0)).astype(jnp.int32))
    result = 0
    for level in LEVELS:
        fits = longest <= SHORT
        for need, size in zip(needs, level[1:]):
            fits = fits & (need <= size)
        result = result + jnp.where(fits, 0, 1)
    choice[0] = result + jnp.where(longest <= SHORT, 0, 1)


def shards(
    hidden, queries, new_key, new_value, cache_keys, cache_values, w_out, lengths, moved_slot
):
    slots, cap, width = cache_keys.shape
    any_spec = pl.BlockSpec(memory_space=pl.ANY)
    vmem_spec = pl.BlockSpec(memory_space=pltpu.VMEM)
    smem_spec = pl.BlockSpec(memory_space=pltpu.SMEM)

    choice = pl.pallas_call(
        choose_kernel,
        out_shape=jax.ShapeDtypeStruct((1,), jnp.int32),
        in_specs=[vmem_spec] * 2,
        out_specs=smem_spec,
        name="choose",
    )(lengths.reshape(1, -1), moved_slot.reshape(1, -1))

    builds = [functools.partial(move, CHUNKS, level, i) for i, level in enumerate(LEVELS)]
    builds.append(functools.partial(move, CHUNKS, DIRECT, len(builds)))
    builds.append(functools.partial(move, WHOLE, DIRECT, len(builds)))
    small, arrived = lax.switch(
        choice[0], builds,
        lengths, moved_slot, hidden, queries, new_key, new_value, cache_keys, cache_values, w_out,
    )

    return pl.pallas_call(
        place_kernel,
        out_shape=(
            jax.ShapeDtypeStruct((slots, w_out.shape[1] // 4), jnp.bfloat16),
            jax.ShapeDtypeStruct(cache_keys.shape, cache_keys.dtype),
            jax.ShapeDtypeStruct(cache_keys.shape, cache_keys.dtype),
        ),
        in_specs=[smem_spec] * 2 + [vmem_spec] * 3 + [any_spec] * 3,
        out_specs=(vmem_spec, any_spec, any_spec),
        scratch_shapes=[
            pltpu.VMEM((PART, width), jnp.bfloat16),
            pltpu.VMEM((slots, 2, cap, width), jnp.bfloat16),
            pltpu.SemaphoreType.DMA((4 * cap // PART,)),
            pltpu.SemaphoreType.DMA((4 * cap // PART,)),
        ],
        compiler_params=pltpu.CompilerParams(vmem_limit_bytes=56 * 2**20),
        name="place",
    )(lengths, moved_slot, new_key, new_value, small, cache_keys, cache_values, arrived)


def solution(mesh):
    return jax.shard_map(
        shards,
        mesh=mesh,
        in_specs=(
            P("replica", None),
            P("replica", "tensor"),
            P("replica", "tensor"),
            P("replica", "tensor"),
            P("replica", None, "tensor"),
            P("replica", None, "tensor"),
            P("tensor", None),
            P(),
            P(),
        ),
        out_specs=(
            P("replica", "tensor"),
            P("replica", None, "tensor"),
            P("replica", None, "tensor"),
        ),
        check_vma=False,
    )
```

time: 66.4 us -> 59.2 us (0.89)
  Pallas kernels: 64.9 us -> 57.3 us
    pallas_call x1, Pallas kernels: 59 us -> 50.4 us  [move(): pl.pallas_call(functools.partial(move_kernel, chunks, slots), out_shape=(...]
    pallas_call x1, Pallas kernels: 4.4 us -> 5.39 us  [shards(): pl.pallas_call(place_kernel, out_shape=(jax.ShapeDtypeStruct((slots, w_ou...]
where the time goes in v3:
time: 59.2 us; the launch traced here: 59 us
  Pallas kernels  57.3 us (97%)
  between operations  1.47 us (2%)
    pallas_call x1, Pallas kernels, move(): pl.pallas_call(functools.partial(move_kernel, chunks, slots), out_shape=(...  50.4 us
    pallas_call x1, Pallas kernels, shards(): pl.pallas_call(place_kernel, out_shape=(jax.ShapeDtypeStruct((slots, w_ou...  5.39 us
    pallas_call x1, Pallas kernels, shards(): pl.pallas_call(choose_kernel, out_shape=jax.ShapeDtypeStruct((1,), jnp.in...  1.51 us

profile of v3, /device:TPU:24, one launch (start us, length us, event | category | flops | bytes accessed | tf_op | source)
XLA Modules:
  0.0 59.0 jit_solution(17834784958273297545)
XLA Ops:
  0.6 1.5 %choose.1 = s32[1]{0:T(128)} custom-call(s32[1,128]{1,0:T(1,128)} %bitcast.3, s32[1,64]{1,0:T(1,128)} %bitcast.4), custom_call_target="tpu_custom_call" | custom-call | tf_op jit(solution)/shard_map/choose/pallas_call | solution.py:464
  2.8 50.7 %conditional.1 = ((f32[32,128]{1,0:T(8,128)S(1)}, bf16[2,768,512]{2,1,0:T(8,128)(2,1)S(1)})) conditional(s32[]{:T(128)} %bitcast.2, (s32[128]{0:T(128)}, s32[64]{0:T(128)}, bf16[2,4096]{1,0:T(2,128)(2,1)}, bf16[2,512]{1,0:T(2,128)(2,1)}, bf16[2,512]{1,0:T(2,128)(2,1)}, /*index=5*/bf16[2,512]{1,0:T(2,128)(2,1)}, ...), branch_computations={%region_0.0_spmd, %region_1.0_spmd, %region_2.0_spmd, %region_3.0_... | conditional | bytes 8 | solution.py:475
  2.8 50.4 %move1.1 = (f32[32,128]{1,0:T(8,128)S(1)}, bf16[2,768,512]{2,1,0:T(8,128)(2,1)S(1)}) custom-call(s32[128]{0:T(128)} %get-tuple-element.99.lengths, s32[64]{0:T(128)} %get-tuple-element.100.moved, bf16[2,4096]{1,0:T(2,128)(2,1)} %get-tuple-element.101.hidden, bf16[2,512]{1,0:T(2,128)(2,1)} %get-tuple-element.102.queries, ...), custom_call_target="tpu_custom_call" | custom-call | tf_op jit(solution)/shard_map/cond/branch_1_fun/move1/pallas_call | solution.py:321
  53.5 5.4 %place.1 = (bf16[2,1024]{1,0:T(2,128)(2,1)}, bf16[2,768,512]{2,1,0:T(8,128)(2,1)}, bf16[2,768,512]{2,1,0:T(8,128)(2,1)}) custom-call(s32[128]{0:T(128)} %lengths.1, s32[64]{0:T(128)} %moved.1, bf16[2,512]{1,0:T(2,128)(2,1)} %new_key.1, bf16[2,512]{1,0:T(2,128)(2,1)} %new_value.1, f32[32,128]{1,0:T(8,128)S(1)} %get-tuple-element.140.small, ...), custom_call_target="tpu_custom_call" | custom-call | tf_op jit(solution)/shard_map/place/pallas_call | solution.py:480

commit v4 on v3

v4 whole, which is shorter than its diff:
```python
import functools

import jax
import jax.numpy as jnp
from jax import lax
from jax.experimental import pallas as pl
from jax.experimental.pallas import tpu as pltpu
from jax.sharding import PartitionSpec as P

HEAD_DIM = 128
TILE = 16
LANES = 256
MESH = pl.DeviceIdType.MESH

OFFSETS = tuple((dx, dy) for dx in range(4) for dy in range(4))
K = len(OFFSETS)
STEP = K // 4
SHORT = 36
CHUNKS = ((0, 1), (1, 4), (4, 6), (6, 9))
LEVELS = ((0, 20, 10, 10), (0, 23, 12, 12), (0, 26, 14, 15), (0, 34, 18, 18))
DIRECT = (0, 0, 0, 0)
WHOLE = ((0, 3), (3, 6), (6, 9), (9, 12))
ORDER = (
    ("attend",), ("along", 1), ("settle",), ("back", 1), ("along", 2), ("finish",), ("land", 0),
    ("back", 2), ("along", 3), ("land", 1), ("back", 3), ("land", 2), ("land", 3),
)
PLAIN = (("attend",), ("settle",), ("finish",), ("land", 0), ("land", 1), ("land", 2), ("land", 3))
SPLIT = 256


def block_diagonal(row, heads):
    width = row.shape[1]
    row_id = lax.broadcasted_iota(jnp.int32, (8, width), 0)
    col_id = lax.broadcasted_iota(jnp.int32, (8, width), 1)
    own = (col_id >= row_id * HEAD_DIM) & (col_id < row_id * HEAD_DIM + HEAD_DIM)
    return own, jnp.where(own, jnp.broadcast_to(row, (8, width)), 0.0)


def attend_row(query, fresh_key, fresh_value, keys_ref, values_ref, length):
    width = keys_ref.shape[1]
    own, query_block = block_diagonal(query, width // HEAD_DIM)
    scale = HEAD_DIM**-0.5
    scores = lax.dot_general(
        query_block.astype(jnp.bfloat16), keys_ref[...], (((1,), (1,)), ((), ())), preferred_element_type=jnp.float32
    )
    scores = scores * scale
    fresh_score = jnp.sum(query_block * fresh_key, axis=1, keepdims=True) * scale
    position = lax.broadcasted_iota(jnp.int32, scores.shape, 1)
    live = position < length
    peak = jnp.maximum(jnp.max(jnp.where(live, scores, -1e30), axis=1, keepdims=True), fresh_score)
    terms = jnp.where(live, jnp.exp(jnp.minimum(scores - peak, 0.0)), 0.0)
    fresh_term = jnp.exp(fresh_score - peak)
    total = jnp.sum(terms, axis=1, keepdims=True) + fresh_term
    weights = (terms / total).astype(jnp.bfloat16)
    fresh_weight = (fresh_term / total).astype(jnp.bfloat16).astype(jnp.float32)
    mixed = lax.dot_general(
        weights, values_ref[...], (((1,), (0,)), ((), ())), preferred_element_type=jnp.float32
    )
    mixed = mixed + fresh_weight * fresh_value
    return jnp.sum(jnp.where(own, mixed, 0.0), axis=0, keepdims=True)


def as_rows(two_rows):
    count = two_rows.shape[1] // 128
    pieces = [two_rows[s : s + 1, j * 128 : (j + 1) * 128] for s in range(2) for j in range(count)]
    return jnp.concatenate(pieces, axis=0)


def as_line(rows):
    return jnp.concatenate([rows[j : j + 1, :] for j in range(rows.shape[0])], axis=1)


def replica_at(plane, x, y):
    return plane * 16 + (x % 4) * 4 + y % 4


def move_kernel(
    chunks, slots,
    lengths, moved, hidden, queries, new_key, new_value, cache_keys, cache_values, w_out,
    small_out, settled,
    keys, values, weights, partial, partial_in, fresh_out, fresh_in,
    load_sem, part_send, part_recv, along_send, along_recv, out_send, out_recv, back_send, back_recv, store_sem,
    *buffers,
):
    count = len(chunks)
    outgoing, buffers = buffers[:count], buffers[count:]
    final, buffers = buffers[:count], buffers[count:]
    held, packed, unpacked, back = {}, {}, {}, {}
    spread = [c for c in range(count) if slots[c]]
    for i, c in enumerate(spread):
        held[c], packed[c], unpacked[c], back[c] = buffers[i * 4 : i * 4 + 4]
    replica = lax.axis_index("replica")
    tensor = lax.axis_index("tensor")
    plane, x, y = replica // 16, (replica // 4) % 4, replica % 4
    partner = (replica + 32) % 64

    loads = []
    parts = [(cache, held_rows, span) for span in (slice(0, SPLIT), slice(SPLIT, None)) for cache, held_rows in ((cache_keys, keys), (cache_values, values))]
    for i, (cache, held_rows, span) in enumerate(parts):
        loads.append(pltpu.make_async_copy(cache.at[:, span], held_rows.at[:, span], load_sem.at[i]))
    loads.append(pltpu.make_async_copy(w_out, weights, load_sem.at[4]))
    for load in loads:
        load.start()

    peers = [(replica, (tensor + k) % 4) for k in range(1, 4)]
    peers += [(partner, (tensor + k) % 4) for k in range(4)]
    if spread:
        peers += [(replica_at(plane, x + dx, y + dy), tensor) for dx, dy in OFFSETS[1:]]
    barrier = pltpu.get_barrier_semaphore()
    for peer in peers:
        pl.semaphore_signal(barrier, inc=1, device_id=peer, device_id_type=MESH)

    leaving = moved[replica]

    def items_of(source, k):
        slot = moved[source]
        length = lengths[source * 2 + jnp.maximum(slot, 0)]
        return jnp.where(slot >= 0, ((length + TILE) >> 4) + (STEP - 1 - k // 4) >> (STEP.bit_length() - 1), 0)

    def send(source, target, device, send_sem, recv_sem):
        copy = pltpu.make_async_remote_copy(
            src_ref=source, dst_ref=target, send_sem=send_sem, recv_sem=recv_sem,
            device_id=device, device_id_type=MESH,
        )
        copy.start()
        return copy

    def landing(buffer, sem):
        return pltpu.make_async_remote_copy(
            src_ref=buffer, dst_ref=buffer, send_sem=sem, recv_sem=sem, device_id=(partner, tensor), device_id_type=MESH
        )

    def copy_units(chunk, body):
        def step(item, carry):
            for k in range(K):
                rows = pl.ds(pl.multiple_of((item * STEP + k // 4) * TILE, TILE), TILE)
                lanes = slice(k % 2 * LANES, (k % 2 + 1) * LANES)
                body(k % 4 // 2, rows, lanes, k, item - chunk[0])
            return carry

        lax.fori_loop(chunk[0], chunk[1], step, 0)

    waited = 0
    sent_along = {}
    for c, chunk in enumerate(chunks):
        if c == 0 or (waited == 2 and chunk[1] * STEP * TILE > SPLIT):
            loads[waited].wait()
            loads[waited + 1].wait()
            waited += 2
            if chunk[1] * STEP * TILE > SPLIT and waited == 2:
                loads[2].wait()
                loads[3].wait()
                waited = 4

        def pack(kind, rows, lanes, relay, item, c=c):
            held_rows = (keys, values)[kind]
            outgoing[c][relay, item] = jnp.where(leaving == 1, held_rows[1, rows, lanes], held_rows[0, rows, lanes])

        copy_units(chunk, pack)
        if c == 0:
            pl.semaphore_wait(barrier, len(peers))
        if not slots[c]:
            sent_along[c] = send(outgoing[c], final[c], (partner, tensor), along_send.at[c], along_recv.at[c])
            continue
        depth = chunk[1] - chunk[0]
        for k in range(1, K):
            dx, dy = OFFSETS[k]
            send(
                outgoing[c].at[k], held[c].at[k * depth : (k + 1) * depth],
                (replica_at(plane, x + dx, y + dy), tensor), out_send.at[c], out_recv.at[c],
            )
        for item in range(depth):
            held[c][item] = outgoing[c][0, item]
    if waited == 2:
        loads[2].wait()
        loads[3].wait()

    if spread:
        leave_items = [items_of(replica_at(plane, x - dx, y - dy), k) for k, (dx, dy) in enumerate(OFFSETS)]
        come_items = [items_of(replica_at((plane + 2) % 4, x - dx, y - dy), k) for k, (dx, dy) in enumerate(OFFSETS)]

    def along(c):
        low, high = chunks[c]
        depth = high - low
        landing(held[c].at[depth:], out_recv.at[c]).wait_recv()
        ends, gaps, total = [], [], 0
        for items in leave_items:
            live = jnp.clip(items - low, 0, depth)
            total = total + live
            ends.append(total)
            gaps.append(depth - live)

        def step(group, carry):
            for lane in range(4):
                slot = jnp.minimum(group * 4 + lane, slots[c] - 1)
                place = slot
                for end, gap in zip(ends[:-1], gaps[:-1]):
                    place = place + jnp.where(slot >= end, gap, 0)
                packed[c][slot] = held[c][jnp.minimum(place, K * depth - 1)]
            return carry

        lax.fori_loop(0, -(-slots[c] // 4), step, 0)
        sent_along[c] = send(packed[c], unpacked[c], (partner, tensor), along_send.at[c], along_recv.at[c])

    def spread_back(c):
        sent_along[c].wait_recv()
        low, high = chunks[c]
        starts, total = [], 0
        for items in come_items:
            starts.append(total)
            total = total + jnp.clip(items - low, 0, high - low)
        for k in range(K - 1, -1, -1):
            target = final[c] if k == 0 else back[c]
            for item in range(high - low):
                target[k, item] = unpacked[c][jnp.minimum(starts[k] + item, slots[c] - 1)]
            if k:
                dx, dy = OFFSETS[k]
                send(
                    back[c].at[k], final[c].at[k], (replica_at(plane, x - dx, y - dy), tensor),
                    back_send.at[c], back_recv.at[c],
                )

    query_rows = queries[...].astype(jnp.float32)
    key_rows = new_key[...].astype(jnp.float32)
    value_rows = new_value[...].astype(jnp.float32)
    fresh_out[0:8] = as_rows(key_rows)
    fresh_out[8:16] = as_rows(value_rows)
    shares = []

    def attend():
        attended = []
        for slot in range(2):
            attended.append(
                attend_row(
                    query_rows[slot : slot + 1], key_rows[slot : slot + 1], value_rows[slot : slot + 1],
                    keys.at[slot], values.at[slot], lengths[replica * 2 + slot],
                )
            )
        attended = jnp.concatenate(attended + [jnp.zeros((6, attended[0].shape[1]), jnp.float32)], axis=0)
        attended = attended.astype(jnp.bfloat16)

        loads[4].wait()
        for piece in range(4):
            product = jnp.dot(
                attended, weights[:, piece * 1024 : (piece + 1) * 1024], preferred_element_type=jnp.float32
            )
            partial[piece] = as_rows(product[0:2])
        residual = hidden[:, pl.ds(pl.multiple_of(tensor * 1024, 1024), 1024)].astype(jnp.float32)
        partial[tensor] = partial[tensor] + as_rows(residual)

        shares.append(send(fresh_out, fresh_in, (partner, tensor), part_send.at[0], part_recv.at[0]))
        for k in range(1, 8):
            piece = (tensor + k) % 4
            shares.append(
                send(
                    partial.at[piece], partial_in.at[k], ((replica, partner)[k // 4], piece),
                    part_send.at[k], part_recv.at[k],
                )
            )

    def settle():
        for slot in range(2):
            length = jnp.where(leaving == slot, -1, lengths[replica * 2 + slot])
            for held_rows, fresh_rows in ((keys, key_rows), (values, value_rows)):
                fresh = jnp.broadcast_to(fresh_rows[slot : slot + 1], (TILE, fresh_rows.shape[1]))

                def step(block, carry, slot=slot, length=length, held_rows=held_rows, fresh=fresh):
                    rows = pl.ds(pl.multiple_of(block * TILE, TILE), TILE)
                    position = in_block + block * TILE
                    tile = held_rows[slot, rows, :].astype(jnp.float32)
                    tile = jnp.where(position < length, tile, jnp.where(position == length, fresh, 0.0))
                    held_rows[slot, rows, :] = tile.astype(jnp.bfloat16)
                    return carry

                lax.fori_loop(0, keys.shape[1] // TILE, step, 0)

    stores = []

    def store(rows, first_sem):
        for slot in range(2):
            for kind in range(2):
                copy = pltpu.make_async_copy(
                    (keys, values)[kind].at[slot, rows], settled.at[slot, kind, rows],
                    store_sem.at[first_sem + slot * 2 + kind],
                )
                copy.start()
                stores.append(copy)

    def finish():
        for share in shares:
            share.wait()
        here = partial[tensor] + partial_in[1] + partial_in[2] + partial_in[3]
        there = partial_in[4] + partial_in[5] + partial_in[6] + partial_in[7]
        coming = jnp.where(moved[partner] == 1, there[8:16], there[0:8])
        for slot in range(2):
            small_out[slot * 8 : slot * 8 + 8] = jnp.where(leaving == slot, coming, here[slot * 8 : slot * 8 + 8])
        for kind in range(2):
            first, second = fresh_in[kind * 8 : kind * 8 + 4], fresh_in[kind * 8 + 4 : kind * 8 + 8]
            come_fresh.append(as_line(jnp.where(moved[partner] == 1, second, first)))

    come_fresh = []
    come_length = lengths[partner * 2 + jnp.maximum(moved[partner], 0)]
    in_block = lax.broadcasted_iota(jnp.int32, (TILE, keys.shape[2]), 0)
    in_tile = lax.broadcasted_iota(jnp.int32, (TILE, LANES), 0)

    def land(c):
        chunk = chunks[c]
        if slots[c]:
            landing(final[c].at[1:], back_recv.at[c]).wait_recv()
        else:
            sent_along[c].wait_recv()

        def unpack(kind, rows, lanes, relay, item):
            position = in_tile + (item + chunk[0]) * (STEP * TILE) + relay // 4 * TILE
            fresh = jnp.broadcast_to(come_fresh[kind][:, lanes], (TILE, LANES))
            tile = final[c][relay, item].astype(jnp.float32)
            tile = jnp.where(position < come_length, tile, jnp.where(position == come_length, fresh, 0.0))
            tile = tile.astype(jnp.bfloat16)
            held_rows = (keys, values)[kind]
            for slot in range(2):
                held_rows[slot, rows, lanes] = jnp.where(leaving == slot, tile, held_rows[slot, rows, lanes])

        copy_units(chunk, unpack)
        store(slice(chunk[0] * STEP * TILE, chunk[1] * STEP * TILE), 4 * c)

    def settle_rest():
        settle()
        bottom = chunks[-1][1] * STEP * TILE
        if bottom < keys.shape[1]:
            store(slice(bottom, keys.shape[1]), 4 * count)

    steps = {"along": along, "attend": attend, "settle": settle_rest, "finish": finish, "back": spread_back, "land": land}
    for step, *chunk in ORDER if spread else PLAIN:
        steps[step](*chunk)
    for copy in sent_along.values():
        copy.wait_send()
    for c in spread:
        landing(outgoing[c].at[1:], out_send.at[c]).wait_send()
        landing(back[c].at[1:], back_send.at[c]).wait_send()
    for copy in stores:
        copy.wait()


def move(chunks, slots, collective_id, *operands):
    cache_keys, w_out = operands[6], operands[8]
    here, cap, width = cache_keys.shape
    count = len(chunks)
    any_spec = pl.BlockSpec(memory_space=pl.ANY)
    vmem_spec = pl.BlockSpec(memory_space=pltpu.VMEM)
    smem_spec = pl.BlockSpec(memory_space=pltpu.SMEM)

    def items(chunk):
        return pltpu.VMEM((K, chunk[1] - chunk[0], TILE, LANES), jnp.bfloat16)

    buffers = [items(chunk) for chunk in chunks] * 2
    for chunk, size in zip(chunks, slots):
        if size:
            on_the_way = pltpu.VMEM((size, TILE, LANES), jnp.bfloat16)
            flat = pltpu.VMEM((K * (chunk[1] - chunk[0]), TILE, LANES), jnp.bfloat16)
            buffers += [flat, on_the_way, on_the_way, items(chunk)]
    return pl.pallas_call(
        functools.partial(move_kernel, chunks, slots),
        out_shape=(
            jax.ShapeDtypeStruct((16, 128), jnp.float32),
            jax.ShapeDtypeStruct((here, 2, cap, width), jnp.bfloat16),
        ),
        in_specs=[smem_spec] * 2 + [vmem_spec] * 4 + [any_spec] * 3,
        out_specs=(vmem_spec, any_spec),
        scratch_shapes=[
            pltpu.VMEM((here, cap, width), jnp.bfloat16),
            pltpu.VMEM((here, cap, width), jnp.bfloat16),
            pltpu.VMEM(w_out.shape, jnp.bfloat16),
            pltpu.VMEM((4, 16, 128), jnp.float32),
            pltpu.VMEM((8, 16, 128), jnp.float32),
            pltpu.VMEM((16, 128), jnp.float32),
            pltpu.VMEM((16, 128), jnp.float32),
            pltpu.SemaphoreType.DMA((5,)),
            pltpu.SemaphoreType.DMA((8,)),
            pltpu.SemaphoreType.DMA((8,)),
            pltpu.SemaphoreType.DMA((count,)),
            pltpu.SemaphoreType.DMA((count,)),
            pltpu.SemaphoreType.DMA((count,)),
            pltpu.SemaphoreType.DMA((count,)),
            pltpu.SemaphoreType.DMA((count,)),
            pltpu.SemaphoreType.DMA((count,)),
            pltpu.SemaphoreType.DMA((4 * count + 4,)),
            *buffers,
        ],
        compiler_params=pltpu.CompilerParams(
            collective_id=collective_id, has_side_effects=True, vmem_limit_bytes=56 * 2**20
        ),
        name="move%d" % collective_id,
    )(*operands)


def place_kernel(small, settled, layer_out, keys_out, values_out, sems):
    copies = []
    for slot in range(2):
        for kind, target in enumerate((keys_out, values_out)):
            copy = pltpu.make_async_copy(settled.at[slot, kind], target.at[slot], sems.at[slot * 2 + kind])
            copy.start()
            copies.append(copy)
    layer_out[...] = jnp.concatenate([as_line(small[0:8]), as_line(small[8:16])], axis=0).astype(jnp.bfloat16)
    for copy in copies:
        copy.wait()


def choose_kernel(lengths, moved, choice):
    row = lax.broadcasted_iota(jnp.int32, (64, 64), 0)
    col = lax.broadcasted_iota(jnp.int32, (64, 64), 1)
    slot = jnp.sum(jnp.where(row == col, moved[...].astype(jnp.float32), 0.0), axis=1, keepdims=True)
    moves = slot >= 0.0
    wide_row = lax.broadcasted_iota(jnp.int32, (64, 128), 0)
    wide_col = lax.broadcasted_iota(jnp.int32, (64, 128), 1)
    wanted = wide_col.astype(jnp.float32) == 2.0 * wide_row.astype(jnp.float32) + jnp.maximum(slot, 0.0)
    length = jnp.sum(jnp.where(wanted, lengths[...].astype(jnp.float32), 0.0), axis=1, keepdims=True)
    blocks = jnp.where(moves, jnp.floor((length + TILE) * (1.0 / TILE)), 0.0)
    longest = jnp.max(blocks).astype(jnp.int32)
    relays = []
    for first in range(STEP):
        some = row < 0
        for dx, dy in OFFSETS[first * 4 : first * 4 + 4]:
            there = (row & 48) + ((((row >> 2) + dx) & 3) << 2) + ((row + dy) & 3)
            some = some | (there == col)
        relays.append((some, jnp.floor((blocks + (STEP - 1 - first)) * (1.0 / STEP))))
    needs = []
    for low, high in CHUNKS[1:]:
        load = 0.0
        for some, items in relays:
            live = jnp.clip(items - low, 0.0, float(high - low))
            load = load + jnp.where(some, live, 0.0)
        needs.append(jnp.max(jnp.sum(load, axis=0)).astype(jnp.int32))
    result = 0
    for level in LEVELS:
        fits = longest <= SHORT
        for need, size in zip(needs, level[1:]):
            fits = fits & (need <= size)
        result = result + jnp.where(fits, 0, 1)
    choice[0] = result + jnp.where(longest <= SHORT, 0, 1)


def shards(
    hidden, queries, new_key, new_value, cache_keys, cache_values, w_out, lengths, moved_slot
):
    slots, cap, width = cache_keys.shape
    any_spec = pl.BlockSpec(memory_space=pl.ANY)
    vmem_spec = pl.BlockSpec(memory_space=pltpu.VMEM)
    smem_spec = pl.BlockSpec(memory_space=pltpu.SMEM)

    choice = pl.pallas_call(
        choose_kernel,
        out_shape=jax.ShapeDtypeStruct((1,), jnp.int32),
        in_specs=[vmem_spec] * 2,
        out_specs=smem_spec,
        name="choose",
    )(lengths.reshape(1, -1), moved_slot.reshape(1, -1))

    builds = [functools.partial(move, CHUNKS, level, i) for i, level in enumerate(LEVELS)]
    builds.append(functools.partial(move, CHUNKS, DIRECT, len(builds)))
    builds.append(functools.partial(move, WHOLE, DIRECT, len(builds)))
    small, settled = lax.switch(
        choice[0], builds,
        lengths, moved_slot, hidden, queries, new_key, new_value, cache_keys, cache_values, w_out,
    )

    return pl.pallas_call(
        place_kernel,
        out_shape=(
            jax.ShapeDtypeStruct((slots, w_out.shape[1] // 4), jnp.bfloat16),
            jax.ShapeDtypeStruct(cache_keys.shape, cache_keys.dtype),
            jax.ShapeDtypeStruct(cache_keys.shape, cache_keys.dtype),
        ),
        in_specs=[vmem_spec, any_spec],
        out_specs=(vmem_spec, any_spec, any_spec),
        scratch_shapes=[pltpu.SemaphoreType.DMA((4,))],
        name="place",
    )(small, settled)


def solution(mesh):
    return jax.shard_map(
        shards,
        mesh=mesh,
        in_specs=(
            P("replica", None),
            P("replica", "tensor"),
            P("replica", "tensor"),
            P("replica", "tensor"),
            P("replica", None, "tensor"),
            P("replica", None, "tensor"),
            P("tensor", None),
            P(),
            P(),
        ),
        out_specs=(
            P("replica", "tensor"),
            P("replica", None, "tensor"),
            P("replica", None, "tensor"),
        ),
        check_vma=False,
    )
```

time: 59.2 us -> 50.8 us (0.86)
  Pallas kernels: 57.3 us -> 48.7 us
    pallas_call x1, Pallas kernels: 50.4 us -> 44.8 us  [move(): pl.pallas_call(functools.partial(move_kernel, chunks, slots), out_shape=(...]
    pallas_call x1, Pallas kernels: 5.39 us -> 2.28 us  [shards(): pl.pallas_call(place_kernel, out_shape=(jax.ShapeDtypeStruct((slots, w_ou...]
where the time goes in v4:
time: 50.8 us; the launch traced here: 50.4 us
  Pallas kernels  48.7 us (96%)
  between operations  1.47 us (3%)
    pallas_call x1, Pallas kernels, move(): pl.pallas_call(functools.partial(move_kernel, chunks, slots), out_shape=(...  44.8 us
    pallas_call x1, Pallas kernels, shards(): pl.pallas_call(place_kernel, out_shape=(jax.ShapeDtypeStruct((slots, w_ou...  2.28 us
    pallas_call x1, Pallas kernels, shards(): pl.pallas_call(choose_kernel, out_shape=jax.ShapeDtypeStruct((1,), jnp.in...  1.57 us

profile of v4, /device:TPU:24, one launch (start us, length us, event | category | flops | bytes accessed | tf_op | source)
XLA Modules:
  0.0 50.4 jit_solution(10106185998886997033)
XLA Ops:
  0.6 1.6 %choose.1 = s32[1]{0:T(128)} custom-call(s32[1,128]{1,0:T(1,128)} %bitcast.3, s32[1,64]{1,0:T(1,128)} %bitcast.4), custom_call_target="tpu_custom_call" | custom-call | tf_op jit(solution)/shard_map/choose/pallas_call | solution.py:450
  2.9 45.1 %conditional.1 = ((f32[16,128]{1,0:T(8,128)S(1)}, bf16[2,2,768,512]{3,2,1,0:T(8,128)(2,1)S(1)})) conditional(s32[]{:T(128)} %bitcast.2, (s32[128]{0:T(128)}, s32[64]{0:T(128)}, bf16[2,4096]{1,0:T(2,128)(2,1)}, bf16[2,512]{1,0:T(2,128)(2,1)}, bf16[2,512]{1,0:T(2,128)(2,1)}, /*index=5*/bf16[2,512]{1,0:T(2,128)(2,1)}, ...), branch_computations={%region_0.0_spmd, %region_1.0_spmd, %region_2.0_spmd, %region_3.0_... | conditional | bytes 8 | solution.py:461
  2.9 44.8 %move0.1 = (f32[16,128]{1,0:T(8,128)S(1)}, bf16[2,2,768,512]{3,2,1,0:T(8,128)(2,1)S(1)}) custom-call(s32[128]{0:T(128)} %get-tuple-element.108.lengths, s32[64]{0:T(128)} %get-tuple-element.109.moved, bf16[2,4096]{1,0:T(2,128)(2,1)} %get-tuple-element.110.hidden, bf16[2,512]{1,0:T(2,128)(2,1)} %get-tuple-element.111.queries, ...), custom_call_target="tpu_custom_call" | custom-call | tf_op jit(solution)/shard_map/cond/branch_0_fun/move0/pallas_call | solution.py:361
  47.9 2.3 %place.1 = (bf16[2,1024]{1,0:T(2,128)(2,1)}, bf16[2,768,512]{2,1,0:T(8,128)(2,1)}, bf16[2,768,512]{2,1,0:T(8,128)(2,1)}) custom-call(f32[16,128]{1,0:T(8,128)S(1)} %get-tuple-element.167.small, bf16[2,2,768,512]{3,2,1,0:T(8,128)(2,1)S(1)} %get-tuple-element.168.settled), custom_call_target="tpu_custom_call" | custom-call | tf_op jit(solution)/shard_map/place/pallas_call | solution.py:466

commit v5 on v4

--- a/solution.py
+++ b/solution.py
@@ -17,7 +17,7 @@
 STEP = K // 4
 SHORT = 36
 CHUNKS = ((0, 1), (1, 4), (4, 6), (6, 9))
-LEVELS = ((0, 20, 10, 10), (0, 23, 12, 12), (0, 26, 14, 15), (0, 34, 18, 18))
+LEVELS = ((0, 23, 12, 12), (0, 25, 14, 14), (0, 28, 15, 15), (0, 31, 17, 17), (0, 34, 18, 18))
 DIRECT = (0, 0, 0, 0)
 WHOLE = ((0, 3), (3, 6), (6, 9), (9, 12))
 ORDER = (

time: 50.8 us -> 58.8 us (1.16); the launches traced: 50.4 us -> 57.8 us
  Pallas kernels: 48.7 us -> 55.6 us
    pallas_call x1, Pallas kernels: 44.8 us -> 51.7 us  [move(): pl.pallas_call(functools.partial(move_kernel, chunks, slots), out_shape=(...]
where the time goes in v5:
time: 58.8 us; the launch traced here: 57.8 us
  Pallas kernels  55.6 us (95%)
  between operations  1.47 us (2%)
  loops' own time  0.73 us (1%)
    pallas_call x1, Pallas kernels, move(): pl.pallas_call(functools.partial(move_kernel, chunks, slots), out_shape=(...  51.7 us
    pallas_call x1, Pallas kernels, shards(): pl.pallas_call(place_kernel, out_shape=(jax.ShapeDtypeStruct((slots, w_ou...  2.28 us
    pallas_call x1, Pallas kernels, shards(): pl.pallas_call(choose_kernel, out_shape=jax.ShapeDtypeStruct((1,), jnp.in...  1.57 us

profile of v5, /device:TPU:24, one launch (start us, length us, event | category | flops | bytes accessed | tf_op | source)
XLA Modules:
  0.0 57.8 jit_solution(2662156237770058751)
XLA Ops:
  0.6 1.6 %choose.1 = s32[1]{0:T(128)} custom-call(s32[1,128]{1,0:T(1,128)} %bitcast.3, s32[1,64]{1,0:T(1,128)} %bitcast.4), custom_call_target="tpu_custom_call" | custom-call | tf_op jit(solution)/shard_map/choose/pallas_call | solution.py:450
  2.9 52.5 %conditional.1 = ((f32[16,128]{1,0:T(8,128)S(1)}, bf16[2,2,768,512]{3,2,1,0:T(8,128)(2,1)S(1)})) conditional(s32[]{:T(128)} %bitcast.2, (s32[128]{0:T(128)}, s32[64]{0:T(128)}, bf16[2,4096]{1,0:T(2,128)(2,1)}, bf16[2,512]{1,0:T(2,128)(2,1)}, bf16[2,512]{1,0:T(2,128)(2,1)}, /*index=5*/bf16[2,512]{1,0:T(2,128)(2,1)}, ...), branch_computations={%region_0.0_spmd, %region_1.0_spmd, %region_2.0_spmd, %region_3.0_... | conditional | bytes 8 | solution.py:461
  3.1 51.7 %move3.1 = (f32[16,128]{1,0:T(8,128)S(1)}, bf16[2,2,768,512]{3,2,1,0:T(8,128)(2,1)S(1)}) custom-call(s32[128]{0:T(128)} %get-tuple-element.153.lengths, s32[64]{0:T(128)} %get-tuple-element.154.moved, bf16[2,4096]{1,0:T(2,128)(2,1)} %get-tuple-element.155.hidden, bf16[2,512]{1,0:T(2,128)(2,1)} %get-tuple-element.156.queries, ...), custom_call_target="tpu_custom_call" | custom-call | tf_op jit(solution)/shard_map/cond/branch_3_fun/move3/pallas_call | solution.py:361
  55.3 2.3 %place.1 = (bf16[2,1024]{1,0:T(2,128)(2,1)}, bf16[2,768,512]{2,1,0:T(8,128)(2,1)}, bf16[2,768,512]{2,1,0:T(8,128)(2,1)}) custom-call(f32[16,128]{1,0:T(8,128)S(1)} %get-tuple-element.194.small, bf16[2,2,768,512]{3,2,1,0:T(8,128)(2,1)S(1)} %get-tuple-element.195.settled), custom_call_target="tpu_custom_call" | custom-call | tf_op jit(solution)/shard_map/place/pallas_call | solution.py:466
